TPU v7x, 256 devices: a whole 4x4x8 slice. The times are simulated.
256 devices in a mesh: cell: 16 (over x, y), gene: 16 (over z, core).
Axes of the slice: x: 4, y: 4, z: 8, core: 2. Of those that a mesh axis runs over, the one named last changes fastest.
Arguments:
- expression: bfloat16 [4096, 20480], P('cell', 'gene'), may hold values from -12 to 12
- mixing: bfloat16 [4, 256, 512], replicated, may hold values from -0.25 to 0.25
Outputs:
- basis: float32 [256, 20480], P(None, 'gene')
- scores: float32 [4096, 256], P('cell', 'gene')
All inputs are finite; a program needn't handle non-finite values.
Results may differ from a plain program's by a relative error of at most 0.0006.
Values sent between devices are 32-bit elements; how exact they have to be, the bound alone decides.
A program may use at most 64 MiB of HBM per device.

v0:
```python
import jax
import jax.numpy as jnp
from jax import lax
from jax.sharding import PartitionSpec as P

GENES = 20480
NS_ITERS = 8


HIGH = lax.Precision.HIGHEST


def swapped(block, axis, distance):
    count = lax.axis_size(axis)
    route = []
    for low in range(count):
        high = low | 1 << distance
        if high != low and high < count:
            route += [(low, high), (high, low)]
    return lax.ppermute(block, axis, route)


def inner(left, right):
    return lax.dot_general(
        left, right, (((1,), (1,)), ((), ())), precision=HIGH, preferred_element_type=jnp.float32
    )


def product(left, right):
    return jnp.dot(left, right, precision=HIGH, preferred_element_type=jnp.float32)


def compressor(gram_full, mix):
    total = jnp.sqrt(jnp.sum(gram_full * gram_full) + 1e-06)
    eye = jnp.eye(gram_full.shape[0], dtype=jnp.float32)
    resid = eye - gram_full / total
    filt = eye - 0.5 * product(resid, resid)
    return product(mix.astype(jnp.float32), filt)


def stacked_shrink(stacked, mix):
    gram_full = lax.psum(inner(stacked, stacked), "gene")
    return product(compressor(gram_full, mix), stacked)


def on_device(expression, mixing):
    cells = expression.shape[0]
    ell = mixing.shape[1]
    folds = cells // ell - 1
    levels = lax.axis_size("cell").bit_length() - 1
    position = lax.axis_index("cell")
    sketch = expression.astype(jnp.float32)
    for level in range(levels):
        partner = swapped(sketch, "cell", level)
        is_low = position // 2**level % 2 == 0
        upper = jnp.where(is_low, sketch, partner)
        lower = jnp.where(is_low, partner, sketch)
        sketch = stacked_shrink(jnp.concatenate([upper, lower], axis=0), mixing[folds + level])
    gram_final = lax.psum(inner(sketch, sketch), "gene")
    total = jnp.sqrt(jnp.sum(gram_final * gram_final) + 1e-06)
    eye = jnp.eye(ell, dtype=jnp.float32)
    ymat = gram_final / total
    zmat = eye
    for step in range(NS_ITERS):
        middle = 0.5 * (3.0 * eye - product(zmat, ymat))
        ymat = product(ymat, middle)
        zmat = product(middle, zmat)
    basis = jnp.sqrt(jnp.float32(GENES)) * product(zmat, sketch) / jnp.sqrt(total)
    partial_scores = inner(expression.astype(jnp.float32), basis)
    shares = lax.psum_scatter(partial_scores, "gene", scatter_dimension=1, tiled=True)
    squares = lax.psum(jnp.sum(shares * shares, axis=0), "cell")
    spread = squares / jnp.float32(cells * lax.axis_size("cell"))
    scores = shares / jnp.sqrt(spread + 1e-05)
    return (basis, scores)


def solution(mesh):
    placed = (P("cell", "gene"), P())
    return jax.shard_map(
        on_device,
        mesh=mesh,
        in_specs=placed,
        out_specs=(P(None, "gene"), P("cell", "gene")),
        check_vma=False,
    )
```

profile of v0, /device:TPU:1, one launch (start us, length us, event | category | flops | bytes accessed | tf_op | source)
XLA Modules:
  0.0 879.4 jit_solution(5512782284058498139)
XLA Ops:
  7.2 1.2 convert_element_type.30
  8.5 2.2 collective-permute-start
  10.7 27.3 %collective-permute-done = f32[256,1280]{1,0:T(8,128)} collective-permute-done((f32[256,1280]{1,0:T(8,128)S(1)}, f32[256,1280]{1,0:T(8,128)}, u32[]{:S(2)}, u32[]{:S(2)}) %collective-permute-start) | collective-permute-done | bytes 1310752 | tf_op jit(solution)/shard_map/ppermute | solution.py:20
  37.9 1.5 convert_select_fusion.1
  39.4 5.3 fusion.8
  44.8 116.5 %all-reduce.6.cloned.1.call-done = f32[512,512]{1,0:T(8,128)} async-done(((f32[512,512]{1,0:T(8,128)}), f32[512,512]{1,0:T(8,128)}) %all-reduce.6.cloned.1.call-update) | async-done | bytes 1048592 | tf_op jit(solution)/shard_map/psum | solution.py:42
  161.4 2.1 multiply_reduce_fusion.3
  164.2 3.5 convert_subtract_fusion.6
  167.7 1.9 fusion.31
  169.7 3.4 fusion.7
  173.1 2.9 collective-permute-start.1
  176.0 28.4 %collective-permute-done.1 = f32[256,1280]{1,0:T(8,128)S(1)} collective-permute-done((f32[256,1280]{1,0:T(8,128)}, f32[256,1280]{1,0:T(8,128)S(1)}, u32[]{:S(2)}, u32[]{:S(2)}) %collective-permute-start.1) | collective-permute-done | bytes 1310752 | tf_op jit(solution)/shard_map/ppermute | solution.py:20
  204.4 1.5 broadcast_select_fusion.1
  205.9 1.0 copy-done.1
  206.9 5.4 fusion.6
  212.4 111.7 %all-reduce.8.cloned.1.call-done = f32[512,512]{1,0:T(8,128)} async-done(((f32[512,512]{1,0:T(8,128)}), f32[512,512]{1,0:T(8,128)}) %all-reduce.8.cloned.1.call-update) | async-done | bytes 1048592 | tf_op jit(solution)/shard_map/psum | solution.py:42
  324.1 2.1 multiply_reduce_fusion.2
  326.9 3.5 convert_subtract_fusion.4
  330.4 2.1 fusion.29
  332.5 2.4 fusion.5
  334.9 1.5 collective-permute-start.2
  336.4 28.4 %collective-permute-done.2 = f32[256,1280]{1,0:T(8,128)} collective-permute-done((f32[256,1280]{1,0:T(8,128)S(1)}, f32[256,1280]{1,0:T(8,128)}, u32[]{:S(2)}, u32[]{:S(2)}) %collective-permute-start.2) | collective-permute-done | bytes 1310752 | tf_op jit(solution)/shard_map/ppermute | solution.py:20
  364.7 1.5 broadcast_select_fusion.3
  366.2 1.0 copy-done.3
  367.3 5.4 fusion.4
  372.8 111.6 %all-reduce.10.cloned.1.call-done = f32[512,512]{1,0:T(8,128)} async-done(((f32[512,512]{1,0:T(8,128)}), f32[512,512]{1,0:T(8,128)}) %all-reduce.10.cloned.1.call-update) | async-done | bytes 1048592 | tf_op jit(solution)/shard_map/psum | solution.py:42
  484.4 2.1 multiply_reduce_fusion.1
  487.2 3.5 convert_subtract_fusion.2
  490.8 2.1 fusion.27
  492.8 2.4 fusion.3
  495.2 3.2 collective-permute-start.3
  498.4 28.4 %collective-permute-done.3 = f32[256,1280]{1,0:T(8,128)} collective-permute-done((f32[256,1280]{1,0:T(8,128)S(1)}, f32[256,1280]{1,0:T(8,128)}, u32[]{:S(2)}, u32[]{:S(2)}) %collective-permute-start.3) | collective-permute-done | bytes 1310752 | tf_op jit(solution)/shard_map/ppermute | solution.py:20
  526.8 1.5 broadcast_select_fusion.5
  528.3 1.0 copy-done.5
  529.3 5.4 fusion.2
  534.8 111.6 %all-reduce.12.cloned.1.call-done = f32[512,512]{1,0:T(8,128)} async-done(((f32[512,512]{1,0:T(8,128)}), f32[512,512]{1,0:T(8,128)}) %all-reduce.12.cloned.1.call-update) | async-done | bytes 1048592 | tf_op jit(solution)/shard_map/psum | solution.py:42
  646.4 2.1 multiply_reduce_fusion
  649.2 3.5 convert_subtract_fusion
  652.8 2.1 fusion.25
  654.8 2.4 fusion.1
  657.2 1.9 fusion.47
  659.4 108.8 %all-reduce.14.cloned.1.call-done = f32[256,256]{1,0:T(8,128)} async-done(((f32[256,256]{1,0:T(8,128)}), f32[256,256]{1,0:T(8,128)}) %all-reduce.14.cloned.1.call-update) | async-done | bytes 262160 | tf_op jit(solution)/shard_map/psum | solution.py:59
  768.3 1.7 multiply_reduce_fusion.4
  770.7 1.3 fusion.16
  772.2 0.4 fusion.38
  772.6 0.4 fusion.15
  773.0 0.4 fusion.49
  773.8 0.4 fusion.14
  774.6 0.4 fusion.50
  775.0 0.4 fusion.13
  775.4 0.4 fusion.53
  776.1 0.4 fusion.12
  776.9 0.4 fusion.54
  777.3 0.4 fusion.11
  777.7 0.4 fusion.57
  778.4 0.4 fusion.10
  779.2 0.4 fusion.59
  779.6 0.4 fusion.9
  780.4 1.2 fusion
  781.7 1.5 convolution_bitcast_fusion
  783.1 53.8 %reduce-scatter.2.cloned.1.call-done = f32[256,16]{0,1:T(8,128)} async-done(((f32[256,256]{0,1:T(8,128)}), f32[256,16]{0,1:T(8,128)}) %reduce-scatter.2.cloned.1.call-update) | async-done | bytes 16400 | tf_op jit(solution)/shard_map/reduce_scatter | solution.py:70
  836.9 0.8 multiply_reduce_fusion.5
  837.8 33.2 %psum.47 = f32[16]{0:T(128)S(1)} all-reduce(f32[16]{0:T(128)S(1)} %multiply_reduce_fusion.5), channel_id=1, replica_groups=mesh['cell'=16,'gene'=16] {'cell'}, use_global_device_ids=true, to_apply=%region_12.13 | all-reduce | flops 16 | bytes 128 | tf_op jit(solution)/shard_map/psum | solution.py:71
  871.0 1.4 broadcast_divide_fusion.3
  (36 shorter events, 3.5 us)
Async XLA Ops:
  7.2 30.8 %copy-start = (bf16[256,1280]{1,0:T(8,128)(2,1)S(1)}, bf16[256,1280]{1,0:T(8,128)(2,1)}, u32[]{:S(2)}) copy-start(bf16[256,1280]{1,0:T(8,128)(2,1)} %param.2) | copy-start | bytes 1966084
  7.2 154.2 %all-reduce.6.cloned.1.call-start = ((), (), s32[]{:S(2)}) async-start(), calls=%async_computation.1 | async-start | bytes 2097152 | tf_op jit(solution)/shard_map/psum | solution.py:42
  8.5 29.5 %collective-permute-start = (f32[256,1280]{1,0:T(8,128)S(1)}, f32[256,1280]{1,0:T(8,128)}, u32[]{:S(2)}, u32[]{:S(2)}) collective-permute-start(f32[256,1280]{1,0:T(8,128)S(1)} %convert_element_type.30), channel_id=1, source_target_pairs={{0,16},{16,0},{32,48},{48,32},{64,80},{80,64},{96,112},{112,96},{1... | collective-permute-start | bytes 3932168 | tf_op jit(solution)/shard_map/ppermute | solution.py:20
  44.8 279.3 %all-reduce.8.cloned.1.call-start = ((), (), s32[]{:S(2)}) async-start(), calls=%async_computation.2 | async-start | bytes 2097152 | tf_op jit(solution)/shard_map/psum | solution.py:42
  173.1 31.3 %collective-permute-start.1 = (f32[256,1280]{1,0:T(8,128)}, f32[256,1280]{1,0:T(8,128)S(1)}, u32[]{:S(2)}, u32[]{:S(2)}) collective-permute-start(f32[256,1280]{1,0:T(8,128)} %fusion.7), channel_id=1, source_target_pairs={{0,32},{32,0},{16,48},{48,16},{64,96},{96,64},{80,112},{112,80},{1... | collective-permute-start | bytes 3932168 | tf_op jit(solution)/shard_map/ppermute | solution.py:20
  205.9 1.1 copy-start.1
  212.4 272.0 %all-reduce.10.cloned.1.call-start = ((), (), s32[]{:S(2)}) async-start(), calls=%async_computation.3 | async-start | bytes 2097152 | tf_op jit(solution)/shard_map/psum | solution.py:42
  330.4 2.1 copy-start.2
  334.9 29.9 %collective-permute-start.2 = (f32[256,1280]{1,0:T(8,128)S(1)}, f32[256,1280]{1,0:T(8,128)}, u32[]{:S(2)}, u32[]{:S(2)}) collective-permute-start(f32[256,1280]{1,0:T(8,128)S(1)} %fusion.5), channel_id=1, source_target_pairs={{0,64},{64,0},{16,80},{80,16},{32,96},{96,32},{48,112},{112,48},{1... | collective-permute-start | bytes 3932168 | tf_op jit(solution)/shard_map/ppermute | solution.py:20
  366.2 1.1 copy-start.3
  372.7 273.7 %all-reduce.12.cloned.1.call-start = ((), (), s32[]{:S(2)}) async-start(), calls=%async_computation.4 | async-start | bytes 2097152 | tf_op jit(solution)/shard_map/psum | solution.py:42
  490.7 2.1 copy-start.4
  495.2 31.6 %collective-permute-start.3 = (f32[256,1280]{1,0:T(8,128)S(1)}, f32[256,1280]{1,0:T(8,128)}, u32[]{:S(2)}, u32[]{:S(2)}) collective-permute-start(f32[256,1280]{1,0:T(8,128)S(1)} %fusion.3), channel_id=1, source_target_pairs={{0,128},{128,0},{16,144},{144,16},{32,160},{160,32},{48,176},{176,... | collective-permute-start | bytes 3932168 | tf_op jit(solution)/shard_map/ppermute | solution.py:20
  528.3 1.1 copy-start.5
  534.8 233.5 %all-reduce.14.cloned.1.call-start = ((), (), s32[]{:S(2)}) async-start(), calls=%async_computation.5 | async-start | bytes 524288 | tf_op jit(solution)/shard_map/psum | solution.py:59
  652.8 2.1 copy-start.6
  659.2 177.7 %reduce-scatter.2.cloned.1.call-start = ((), (), s32[]{:S(2)}) async-start(), calls=%async_computation.6 | async-start | bytes 278528 | tf_op jit(solution)/shard_map/reduce_scatter | solution.py:70
  768.3 4.0 copy-start.8
  781.6 90.8 %copy-start.7 = (f32[256,1280]{1,0:T(8,128)}, f32[256,1280]{1,0:T(8,128)S(1)}, u32[]{:S(2)}) copy-start(f32[256,1280]{1,0:T(8,128)S(1)} %fusion) | copy-start | bytes 3932164
Sparse Core Ops, SparseCore 0:
  44.9 116.4 all-reduce.5
  212.5 111.5 all-reduce.7
  372.9 111.5 all-reduce.9
  534.9 111.5 all-reduce.11
  659.3 108.8 all-reduce.13
  783.3 53.6 reduce-scatter.1
where the time goes:
time: 896 us; the launch traced here: 879 us
  waiting for transfers between devices  727 us (81%)
  matrix products  68.5 us (8%)
  blocking collectives  33.2 us (4%)
  other arithmetic  19.5 us (2%)
  between operations  18.2 us (2%)
  starting transfers between devices  10.2 us (1%)
    psum x4, waiting for transfers between devices, stacked_shrink(): gram_full = lax.psum(inner(stacked, stacked), 'gene')  451 us
    ppermute x4, waiting for transfers between devices, swapped(): return lax.ppermute(block, axis, route)  112 us
    psum x1, waiting for transfers between devices, on_device(): gram_final = lax.psum(inner(sketch, sketch), 'gene')  109 us
    reduce_scatter x1, waiting for transfers between devices, on_device(): lax.psum_scatter(partial_scores, 'gene', scatter_dimension=1, tiled=True)  53.8 us
    dot_general x36, matrix products, product(): jnp.dot(left, right, precision=HIGH, preferred_element_type=jnp.float32)  43.5 us
    psum x1, blocking collectives, on_device(): squares = lax.psum(jnp.sum(shares * shares, axis=0), 'cell')  33.2 us
    dot_general x6, matrix products, inner(): lax.dot_general(left, right, (((1,), (1,)), ((), ())), precision=HIGH, pr...  25 us
  transfers between devices with their start and end apart: 10, of which 10 were waited for; matrix products, arithmetic and copies ran while one was open for 0% of the time, Pallas kernels for 0%

commit v1 on v0

v1 whole, which is shorter than its diff:
```python
import jax
import jax.numpy as jnp
from jax import lax
from jax.experimental import pallas as pl
from jax.experimental.pallas import tpu as pltpu
from jax.sharding import PartitionSpec as P

GENES = 20480
CELLS = 4096
ELL = 256
NS_ITERS = 8
NY, NX, NZ = 4, 4, 8
NYZ = NY * NZ
LOCAL = GENES // 16
QUART = LOCAL // NY
PART = LOCAL // 16
MESH = pl.DeviceIdType.MESH
F32 = jnp.float32
BF16 = jnp.bfloat16
NT = (((1,), (1,)), ((), ()))
NN = (((1,), (0,)), ((), ()))
TN = (((0,), (0,)), ((), ()))


def split(a):
    hi = a.astype(BF16)
    return hi, (a - hi.astype(F32)).astype(BF16)


def dot(a, b, dims):
    return lax.dot_general(a, b, dims, preferred_element_type=F32)


def dot2(a, b, dims):
    return dot(a, b[0], dims) + dot(a, b[1], dims)


def dot3(a, b, dims):
    return dot(a[0], b[0], dims) + (dot(a[0], b[1], dims) + dot(a[1], b[0], dims))


def joined(pair):
    return jnp.concatenate([pair[0], pair[1]], axis=1)


def halves(ref, block):
    ref[0] = block[:, :128]
    ref[1] = block[:, 128:]


def kernel(
    x_ref, mix_ref, basis_ref, scores_ref,
    xt, rx, part, corebuf, half, rsbuf, xbuf, total,
    selfp, selfcore, selfhalf, selfrs, selfall,
    low, high, quad, mid, pairbuf2, pairbuf3, pairself, final,
    gh, gl, fh, fl, prod, prodcore, prodhalf, prodrs, sq,
    send_sem, core_sem, rs_sem, ag_sem, cag_sem, x_sem,
    a2a_sem, self_sem, pair_sem, pself_sem, fin_sem, pr_sem, sq_sem,
):
    cell, gene = lax.axis_index("cell"), lax.axis_index("gene")
    x, y = cell // NY, cell % NY
    z, c = gene // 2, gene % 2
    yz = y * NZ + z
    sends = []

    def put(src, dst, send, recv, to):
        copy = pltpu.make_async_remote_copy(
            src_ref=src, dst_ref=dst, send_sem=send, recv_sem=recv,
            device_id=to, device_id_type=MESH,
        )
        copy.start()
        return copy

    def taken(like, sem):
        pltpu.make_async_copy(like, like, sem).wait()

    def sent(like, sem):
        sends.append((like, sem))

    def other(i):
        j = lax.rem(yz + i, NYZ)
        return j, (x * NY + j // NZ, (j % NZ) * 2 + c)

    sibling = (cell, z * 2 + (1 - c))

    barrier = pltpu.get_barrier_semaphore()

    def greet(to):
        pl.semaphore_signal(barrier, inc=1, device_id=to, device_id_type=MESH)

    def greet_yz(i, carry):
        greet(other(i)[1])
        return carry

    lax.fori_loop(1, NYZ, greet_yz, 0)

    def greet_cells(i, carry):
        greet((lax.rem(cell - y + NY * (1 + i // NY), 16) + i % NY, gene))
        return carry

    lax.fori_loop(0, 12, greet_cells, 0)
    greet(sibling)

    for t in range(LOCAL // 128):
        xt[t * 128:(t + 1) * 128, :] = x_ref[:, t * 128:(t + 1) * 128].astype(F32).T
    own = pl.ds(pl.multiple_of(y * QUART, QUART), QUART)
    rx[y] = xt[own, :]
    xb = x_ref[...]
    halves(selfp, dot(xb, xb, NT))
    pl.semaphore_wait(barrier, NYZ - 1 + 12 + 1)

    for i in range(1, NY):
        q = lax.rem(y + i, NY)
        put(
            xt.at[pl.ds(pl.multiple_of(q * QUART, QUART), QUART), :], rx.at[y],
            send_sem.at[0], a2a_sem, (x * NY + q, gene),
        )
    sent(xt.at[pl.ds(0, 3 * QUART), :], send_sem.at[0])

    def rows(base, count):
        return pl.ds(pl.multiple_of(base, count), count)

    mine = rows(c * 128, 128)
    theirs = rows((1 - c) * 128, 128)

    put(selfp.at[:, theirs, :], selfcore, send_sem.at[1], self_sem.at[0], sibling)
    sent(selfcore, send_sem.at[1])
    taken(selfcore, self_sem.at[0])
    selfhalf[...] = selfp[:, mine, :] + selfcore[...]
    for i in range(1, NZ):
        k = lax.rem(z + i, NZ)
        put(
            selfhalf.at[:, rows(k * 16, 16), :], selfrs.at[i - 1],
            send_sem.at[2], self_sem.at[1], (cell, k * 2 + c),
        )
    sent(selfrs, send_sem.at[2])
    taken(selfrs, self_sem.at[1])
    piece = selfhalf[:, rows(z * 16, 16), :]
    for i in range(NZ - 1):
        piece = piece + selfrs[i]
    place = rows(c * 128 + z * 16, 16)
    selfall[y, :, place, :] = piece
    for i in range(1, NZ):
        k = lax.rem(z + i, NZ)
        put(
            selfall.at[y, :, place, :], selfall.at[y, :, place, :],
            send_sem.at[3], self_sem.at[2], (cell, k * 2 + c),
        )
    sent(selfrs, send_sem.at[3])
    taken(selfrs, self_sem.at[2])
    for i in range(1, NY):
        q = lax.rem(y + i, NY)
        put(
            selfall.at[y, :, mine, :], selfall.at[y, :, mine, :],
            send_sem.at[4], self_sem.at[3], (x * NY + q, gene),
        )
    sent(selfall.at[pl.ds(0, 3), :, pl.ds(0, 128), :], send_sem.at[4])

    taken(rx.at[pl.ds(0, 3)], a2a_sem)

    def reduced(level, at, count, planes):
        block = pl.ds(at, count)
        sem = 5 + 5 * level
        put(
            part.at[block, :, theirs, :], corebuf.at[block],
            send_sem.at[sem], core_sem.at[level], sibling,
        )
        sent(corebuf.at[block], send_sem.at[sem])
        taken(corebuf.at[block], core_sem.at[level])
        half[block] = part[block, :, mine, :] + corebuf[block]

        def spread(i, carry):
            j, to = other(i)
            put(
                half.at[block, j // 16, rows((j % 16) * 8, 8), :], rsbuf.at[i - 1, block],
                send_sem.at[sem + 1], rs_sem.at[level], to,
            )
            return carry

        lax.fori_loop(1, NYZ, spread, 0)
        sent(rsbuf.at[:, block], send_sem.at[sem + 1])
        taken(rsbuf.at[:, block], rs_sem.at[level])
        tile = half[block, yz // 16, rows((yz % 16) * 8, 8), :]
        for i in range(NYZ - 1):
            tile = tile + rsbuf[i, block]
        if planes:
            slot = level - 2
            xbuf[slot, x] = tile
            for d in planes:
                to = (x // d % 2 * -2 * d + x + d) if len(planes) == 1 else lax.rem(x + d, NX)
                put(
                    xbuf.at[slot, x], xbuf.at[slot, x],
                    send_sem.at[sem + 2], x_sem.at[slot], (to * NY + y, gene),
                )
            sent(xbuf.at[slot, pl.ds(0, len(planes))], send_sem.at[sem + 2])
            taken(xbuf.at[slot, pl.ds(0, len(planes))], x_sem.at[slot])
            if len(planes) == 1:
                base = x - x % 2
                tile = xbuf[slot, base] + xbuf[slot, base + 1]
            else:
                tile = (xbuf[slot, 0] + xbuf[slot, 1]) + (xbuf[slot, 2] + xbuf[slot, 3])
        spot = rows(c * 128 + (yz % 16) * 8, 8)
        total[block, yz // 16, spot, :] = tile

        def collect(i, carry):
            _, to = other(i)
            piece = total.at[block, yz // 16, spot, :]
            put(piece, piece, send_sem.at[sem + 3], ag_sem.at[level], to)
            return carry

        lax.fori_loop(1, NYZ, collect, 0)
        sent(rsbuf.at[:, block], send_sem.at[sem + 3])
        taken(rsbuf.at[:, block], ag_sem.at[level])
        put(
            total.at[block, :, mine, :], total.at[block, :, mine, :],
            send_sem.at[sem + 4], cag_sem.at[level], sibling,
        )
        sent(corebuf.at[block], send_sem.at[sem + 4])
        taken(corebuf.at[block], cag_sem.at[level])

    def weights(level, lower, cross, upper):
        gram = jnp.concatenate(
            [
                jnp.concatenate([lower, cross], axis=1),
                jnp.concatenate([cross.T, upper], axis=1),
            ],
            axis=0,
        )
        inv = 1.0 / jnp.sqrt(jnp.sum(gram * gram, keepdims=True) + 1e-06)
        hi, lo = split(gram)
        gh[...] = hi
        gl[...] = lo
        mix = mix_ref[level]
        once = dot2(mix, (gh[...], gl[...]), NN)
        twice = dot3(split(once), (gh[...], gl[...]), NN)
        return 0.5 * mix.astype(F32) + once * inv - (0.5 * twice) * (inv * inv)

    def own_gram(w):
        return dot3(split(dot3(w, (gh[...], gl[...]), NN)), w, NT)

    def left(w):
        return w[0][:, :ELL], w[1][:, :ELL]

    def right(w):
        return w[0][:, ELL:], w[1][:, ELL:]

    for p in range(2):
        halves(part.at[p], dot(rx[2 * p].astype(BF16), rx[2 * p + 1].astype(BF16), TN))
    reduced(0, 0, 2, ())
    taken(selfall.at[pl.ds(0, 3), :, pl.ds(0, 128), :], self_sem.at[3])
    put(
        selfall.at[:, :, mine, :], selfall.at[:, :, mine, :],
        send_sem.at[25], self_sem.at[4], sibling,
    )
    sent(selfall.at[:, :, pl.ds(0, 128), :], send_sem.at[25])
    taken(selfall.at[:, :, pl.ds(0, 128), :], self_sem.at[4])
    grams = []
    for p, sketch in ((0, low), (1, high)):
        w = split(weights(0, joined(selfall[2 * p]), joined(total[p]), joined(selfall[2 * p + 1])))
        sketch[...] = dot2(rx[2 * p].astype(BF16), left(w), NT) + dot2(
            rx[2 * p + 1].astype(BF16), right(w), NT
        )
        grams.append(own_gram(w))

    lows, highs = split(low[...]), split(high[...])
    halves(part.at[2], dot3(lows, highs, TN))
    reduced(1, 2, 1, ())
    w = split(weights(1, grams[0], joined(total[2]), grams[1]))
    quad[...] = dot3(lows, left(w), NT) + dot3(highs, right(w), NT)

    for level, step, src, buf, out in ((2, 1, quad, pairbuf2, mid), (3, 2, mid, pairbuf3, None)):
        slot = level - 2
        bit = x // step % 2
        to = ((x + step * (1 - 2 * bit)) * NY + y, gene)
        count = buf.shape[1]
        put(
            src.at[rows((1 - bit) * count, count), :], buf.at[bit],
            send_sem.at[26 + slot], pair_sem.at[slot], to,
        )
        sent(buf.at[0], send_sem.at[26 + slot])
        buf[bit] = src[rows(bit * count, count), :]
        halves(pairself.at[slot, bit], own_gram(w))
        share = pairself.at[slot, bit, :, mine, :]
        put(share, share, send_sem.at[28 + slot], pself_sem.at[slot], to)
        sent(pairself.at[slot, 0, :, pl.ds(0, 128), :], send_sem.at[28 + slot])
        taken(buf.at[0], pair_sem.at[slot])
        lows, highs = split(buf[0]), split(buf[1])
        halves(part.at[level + 1], dot3(lows, highs, TN))
        reduced(level, level + 1, 1, (1,) if level == 2 else (1, 2, 3))
        taken(pairself.at[slot, 0, :, pl.ds(0, 128), :], pself_sem.at[slot])
        across = pairself.at[slot, 1 - bit, :, mine, :]
        put(across, across, send_sem.at[30 + slot], pself_sem.at[2 + slot], sibling)
        sent(pairself.at[slot, 0, :, pl.ds(0, 128), :], send_sem.at[30 + slot])
        taken(pairself.at[slot, 0, :, pl.ds(0, 128), :], pself_sem.at[2 + slot])
        w = split(
            weights(
                level, joined(pairself[slot, 0]), joined(total[level + 1]), joined(pairself[slot, 1])
            )
        )
        sketch = dot3(lows, left(w), NT) + dot3(highs, right(w), NT)
        if out is not None:
            out[...] = sketch

    start = y * QUART + x % 2 * (2 * PART) + x // 2 * PART
    here = final.at[rows(start, PART), :]
    final[rows(start, PART), :] = sketch
    for i in range(1, 16):
        put(here, here, send_sem.at[32], fin_sem, (lax.rem(cell + i, 16), gene))
    sent(final.at[pl.ds(0, 15 * PART), :], send_sem.at[32])

    gram = own_gram(w)
    norm = jnp.sqrt(jnp.sum(gram * gram, keepdims=True) + 1e-06)
    eye = (
        lax.broadcasted_iota(jnp.int32, (ELL, ELL), 0) == lax.broadcasted_iota(jnp.int32, (ELL, ELL), 1)
    ).astype(F32)
    ymat = gram * (1.0 / norm)
    middle = 1.5 * eye - 0.5 * ymat
    zmat = middle
    ymat = dot3(split(ymat), split(middle), NN)

    def refine(step, carry):
        ymat, zmat = split(carry[0]), split(carry[1])
        middle = split(1.5 * eye - 0.5 * dot3(zmat, ymat, NN))
        return dot3(ymat, middle, NN), dot3(middle, zmat, NN)

    ymat, zmat = lax.fori_loop(0, NS_ITERS - 2, refine, (ymat, zmat))
    ymat, zmat = split(ymat), split(zmat)
    middle = split(1.5 * eye - 0.5 * dot3(zmat, ymat, NN))
    scaled = split(dot3(middle, zmat, NN) * (jnp.sqrt(F32(GENES)) / jnp.sqrt(norm)))

    taken(final.at[pl.ds(0, 15 * PART), :], fin_sem)
    hi, lo = split(final[...])
    fh[...] = hi
    fl[...] = lo
    shares = dot2(x_ref[...], (fh[...], fl[...]), NN)
    prod[...] = dot3(scaled, split(shares), NT).reshape(NZ, 2, 16, ELL)

    put(prod.at[:, 1 - c], prodcore, send_sem.at[33], pr_sem.at[0], sibling)
    sent(prodcore, send_sem.at[33])
    taken(prodcore, pr_sem.at[0])
    prodhalf[...] = prod[:, c] + prodcore[...]
    for i in range(1, NZ):
        k = lax.rem(z + i, NZ)
        put(prodhalf.at[k], prodrs.at[i - 1], send_sem.at[34], pr_sem.at[1], (cell, k * 2 + c))
    sent(prodrs, send_sem.at[34])
    basis_ref[...] = dot3(scaled, (fh[...], fl[...]), NT)
    taken(prodrs, pr_sem.at[1])
    scores = prodhalf[z]
    for i in range(NZ - 1):
        scores = scores + prodrs[i]
    sq[cell] = jnp.broadcast_to(jnp.sum(scores * scores, axis=1, keepdims=True), (16, 128))
    for i in range(1, 16):
        put(sq.at[cell], sq.at[cell], send_sem.at[35], sq_sem, (lax.rem(cell + i, 16), gene))
    sent(sq.at[pl.ds(0, 15)], send_sem.at[35])
    taken(sq.at[pl.ds(0, 15)], sq_sem)
    spread = jnp.sum(sq[...], axis=0)[:, :1] * (1.0 / CELLS)
    scores_ref[...] = (scores / jnp.sqrt(spread + 1e-05)).T
    for like, sem in sends:
        taken(like, sem)


def on_device(expression, mixing):
    vmem = pl.BlockSpec(memory_space=pltpu.VMEM)
    dma = pltpu.SemaphoreType.DMA

    def buf(*shape, kind=F32):
        return pltpu.VMEM(shape, kind)

    return pl.pallas_call(
        kernel,
        out_shape=(
            jax.ShapeDtypeStruct((ELL, LOCAL), F32),
            jax.ShapeDtypeStruct((ELL, 16), F32),
        ),
        in_specs=[vmem, vmem],
        out_specs=(vmem, vmem),
        scratch_shapes=[
            buf(LOCAL, ELL), buf(NY, QUART, ELL), buf(5, 2, 256, 128), buf(5, 2, 128, 128),
            buf(5, 2, 128, 128), buf(NYZ - 1, 5, 8, 128), buf(2, NX, 1, 8, 128), buf(5, 2, 256, 128),
            buf(2, 256, 128), buf(2, 128, 128), buf(2, 128, 128), buf(NZ - 1, 2, 16, 128),
            buf(NY, 2, 256, 128),
            buf(QUART, ELL), buf(QUART, ELL), buf(QUART, ELL), buf(2 * PART, ELL),
            buf(2, 2 * PART, ELL), buf(2, PART, ELL), buf(2, 2, 2, 256, 128), buf(LOCAL, ELL),
            buf(2 * ELL, 2 * ELL, kind=BF16), buf(2 * ELL, 2 * ELL, kind=BF16),
            buf(LOCAL, ELL, kind=BF16), buf(LOCAL, ELL, kind=BF16),
            buf(NZ, 2, 16, ELL), buf(NZ, 16, ELL), buf(NZ, 16, ELL), buf(NZ - 1, 16, ELL),
            buf(16, 16, 128),
            dma((36,)), dma((4,)), dma((4,)), dma((4,)), dma((4,)), dma((2,)),
            dma, dma((5,)), dma((2,)), dma((4,)), dma, dma((2,)), dma,
        ],
        compiler_params=pltpu.CompilerParams(
            collective_id=0, has_side_effects=True, vmem_limit_bytes=52 * 2**20
        ),
    )(expression, mixing)


def solution(mesh):
    return jax.shard_map(
        on_device,
        mesh=mesh,
        in_specs=(P("cell", "gene"), P()),
        out_specs=(P(None, "gene"), P("cell", "gene")),
        check_vma=False,
    )
```

time: 896 us -> 173 us (0.19); the launches traced: 879 us -> 173 us
  waiting for transfers between devices: 727 us -> 0 us
  Pallas kernels: 0 us -> 167 us
  matrix products: 68.5 us -> 0 us
  blocking collectives: 33.2 us -> 0 us
  other arithmetic: 19.5 us -> 0 us
  between operations: 18.2 us -> 0.65 us
  starting transfers between devices: 10.2 us -> 0 us
    psum x5 -> x0, waiting for transfers between devices: 560 us -> none  [the longest x4 451 us: stacked_shrink(): gram_full = lax.psum(inner(stacked, stacked), 'gene')]
    pallas_call x0 -> x1, Pallas kernels: none -> 167 us  [on_device(): pl.pallas_call(kernel, out_shape=(jax.ShapeDtypeStruct((ELL, LOCAL), F32)...]
    ppermute x4 -> x0, waiting for transfers between devices: 112 us -> none  [swapped(): return lax.ppermute(block, axis, route)]
    dot_general x42 -> x0, matrix products: 68.5 us -> none  [the longest x36 43.5 us: product(): jnp.dot(left, right, precision=HIGH, preferred_element_type=jnp.float32)]
    reduce_scatter x1 -> x0, waiting for transfers between devices: 53.8 us -> none  [on_device(): lax.psum_scatter(partial_scores, 'gene', scatter_dimension=1, tiled=True)]
    psum x1 -> x0, blocking collectives: 33.2 us -> none  [on_device(): squares = lax.psum(jnp.sum(shares * shares, axis=0), 'cell')]
    reduce_sum x6 -> x0, other arithmetic: 10.9 us -> none  [the longest x4 8.39 us: compressor(): total = jnp.sqrt(jnp.sum(gram_full * gram_full) + 1e-06)]
    ppermute x4 -> x0, starting transfers between devices: 9.77 us -> none  [swapped(): return lax.ppermute(block, axis, route)]
  transfers between devices with their start and end apart: 10 -> 0, of which waited for: 10 -> 0; matrix products, arithmetic and copies ran while one was open for 0% -> 0% of each run, Pallas kernels for 0% -> 0%
where the time goes in v1:
time: 173 us
  Pallas kernels  167 us (97%)
  local copies, waits for them, and re-layouts  5.44 us (3%)
    pallas_call x1, Pallas kernels, on_device(): pl.pallas_call(kernel, out_shape=(jax.ShapeDtypeStruct((ELL, LOCAL), F32)...  167 us
    unnamed x5, local copies, waits for them, and re-layouts  4.76 us

profile of v1, /device:TPU:1, one launch (start us, length us, event | category | flops | bytes accessed | tf_op | source)
XLA Modules:
  0.0 172.8 jit_solution(11248486792320238240)
XLA Ops:
  0.6 0.0 copy-start
  0.6 1.2 copy-done
  1.9 0.0 copy-start.1
  1.9 1.1 copy-done.1
  2.9 166.7 %shard_map.41 = (f32[256,1280]{1,0:T(8,128)}, f32[256,16]{1,0:T(8,128)S(1)}) custom-call(bf16[256,1280]{1,0:T(8,128)(2,1)S(1)} %copy-done.1, bf16[4,256,512]{2,1,0:T(8,128)(2,1)S(1)} %copy-done), custom_call_target="tpu_custom_call" | custom-call | tf_op jit(solution)/shard_map/pallas_call | solution.py:369
  169.6 0.7 copy.4
  170.3 2.5 %copy.6 = f32[256,1280]{1,0:T(8,128)} copy(f32[256,1280]{1,0:T(8,128)} %get-tuple-element.6) | data formatting | bytes 2621440
Async XLA Ops:
  0.6 1.2 copy-start
  1.9 1.1 copy-start.1

commit v2 on v1

--- a/solution.py
+++ b/solution.py
@@ -22,6 +22,28 @@
 TN = (((0,), (0,)), ((), ()))
 
 
+def hops(d, n):
+    return min(d, n - d)
+
+
+ALONG_Y = sorted(range(1, NY), key=lambda d: -hops(d, NY))
+ALONG_Z = sorted(range(1, NZ), key=lambda d: -hops(d, NZ))
+OTHERS = sorted(
+    ((dy, dz) for dy in range(NY) for dz in range(NZ) if dy or dz),
+    key=lambda d: -hops(d[0], NY) - hops(d[1], NZ),
+)
+PLANES = {
+    2: sorted(
+        ((dx, dy) for dx in range(2) for dy in range(NY) if dx or dy),
+        key=lambda d: -d[0] - hops(d[1], NY),
+    ),
+    3: sorted(
+        ((dx, dy) for dx in range(NX) for dy in range(NY) if dx or dy),
+        key=lambda d: -hops(d[0], NX) - hops(d[1], NY),
+    ),
+}
+
+
 def split(a):
     hi = a.astype(BF16)
     return hi, (a - hi.astype(F32)).astype(BF16)
@@ -49,13 +71,13 @@
 
 
 def kernel(
-    x_ref, mix_ref, basis_ref, scores_ref,
-    xt, rx, part, corebuf, half, rsbuf, xbuf, total,
+    x_hbm, mix_hbm, basis_ref, scores_ref,
+    x_ref, mix_ref, xt, rx, part, corebuf, half, rsbuf, cellbuf, zbuf, total,
     selfp, selfcore, selfhalf, selfrs, selfall,
     low, high, quad, mid, pairbuf2, pairbuf3, pairself, final,
     gh, gl, fh, fl, prod, prodcore, prodhalf, prodrs, sq,
-    send_sem, core_sem, rs_sem, ag_sem, cag_sem, x_sem,
-    a2a_sem, self_sem, pair_sem, pself_sem, fin_sem, pr_sem, sq_sem,
+    load_sem, send_sem, core_sem, rs_sem, ag_sem, cag_sem, z_sem,
+    a2a_sem, self_sem, pair_sem, pself_sem, fin_sem, finx_sem, finy_sem, pr_sem, sq_sem,
 ):
     cell, gene = lax.axis_index("cell"), lax.axis_index("gene")
     x, y = cell // NY, cell % NY
@@ -77,10 +99,16 @@
     def sent(like, sem):
         sends.append((like, sem))
 
-    def other(i):
-        j = lax.rem(yz + i, NYZ)
-        return j, (x * NY + j // NZ, (j % NZ) * 2 + c)
-
+    def at(dx, dy, dz):
+        return (lax.rem(x + dx, NX) * NY + lax.rem(y + dy, NY), lax.rem(z + dz, NZ) * 2 + c)
+
+    def paired(dx, dy):
+        return ((x + dx * (1 - 2 * (x % 2))) * NY + lax.rem(y + dy, NY), gene)
+
+    load_x = pltpu.make_async_copy(x_hbm, x_ref, load_sem.at[0])
+    load_mix = pltpu.make_async_copy(mix_hbm, mix_ref, load_sem.at[1])
+    load_x.start()
+    load_mix.start()
     sibling = (cell, z * 2 + (1 - c))
 
     barrier = pltpu.get_barrier_semaphore()
@@ -88,18 +116,13 @@
     def greet(to):
         pl.semaphore_signal(barrier, inc=1, device_id=to, device_id_type=MESH)
 
-    def greet_yz(i, carry):
-        greet(other(i)[1])
-        return carry
-
-    lax.fori_loop(1, NYZ, greet_yz, 0)
-
-    def greet_cells(i, carry):
-        greet((lax.rem(cell - y + NY * (1 + i // NY), 16) + i % NY, gene))
-        return carry
-
-    lax.fori_loop(0, 12, greet_cells, 0)
+    for dy, dz in OTHERS:
+        greet(at(0, dy, dz))
+    for dx, dy in PLANES[3]:
+        if dx:
+            greet(at(dx, dy, 0))
     greet(sibling)
+    load_x.wait()
 
     for t in range(LOCAL // 128):
         xt[t * 128:(t + 1) * 128, :] = x_ref[:, t * 128:(t + 1) * 128].astype(F32).T
@@ -109,7 +132,7 @@
     halves(selfp, dot(xb, xb, NT))
     pl.semaphore_wait(barrier, NYZ - 1 + 12 + 1)
 
-    for i in range(1, NY):
+    for i in ALONG_Y:
         q = lax.rem(y + i, NY)
         put(
             xt.at[pl.ds(pl.multiple_of(q * QUART, QUART), QUART), :], rx.at[y],
@@ -127,7 +150,7 @@
     sent(selfcore, send_sem.at[1])
     taken(selfcore, self_sem.at[0])
     selfhalf[...] = selfp[:, mine, :] + selfcore[...]
-    for i in range(1, NZ):
+    for i in ALONG_Z:
         k = lax.rem(z + i, NZ)
         put(
             selfhalf.at[:, rows(k * 16, 16), :], selfrs.at[i - 1],
@@ -140,7 +163,7 @@
         piece = piece + selfrs[i]
     place = rows(c * 128 + z * 16, 16)
     selfall[y, :, place, :] = piece
-    for i in range(1, NZ):
+    for i in ALONG_Z:
         k = lax.rem(z + i, NZ)
         put(
             selfall.at[y, :, place, :], selfall.at[y, :, place, :],
@@ -148,7 +171,7 @@
         )
     sent(selfrs, send_sem.at[3])
     taken(selfrs, self_sem.at[2])
-    for i in range(1, NY):
+    for i in ALONG_Y:
         q = lax.rem(y + i, NY)
         put(
             selfall.at[y, :, mine, :], selfall.at[y, :, mine, :],
@@ -158,8 +181,8 @@
 
     taken(rx.at[pl.ds(0, 3)], a2a_sem)
 
-    def reduced(level, at, count, planes):
-        block = pl.ds(at, count)
+    def reduced(level, at_block, count):
+        block = pl.ds(at_block, count)
         sem = 5 + 5 * level
         put(
             part.at[block, :, theirs, :], corebuf.at[block],
@@ -168,49 +191,61 @@
         sent(corebuf.at[block], send_sem.at[sem])
         taken(corebuf.at[block], core_sem.at[level])
         half[block] = part[block, :, mine, :] + corebuf[block]
-
-        def spread(i, carry):
-            j, to = other(i)
-            put(
-                half.at[block, j // 16, rows((j % 16) * 8, 8), :], rsbuf.at[i - 1, block],
-                send_sem.at[sem + 1], rs_sem.at[level], to,
-            )
-            return carry
-
-        lax.fori_loop(1, NYZ, spread, 0)
-        sent(rsbuf.at[:, block], send_sem.at[sem + 1])
-        taken(rsbuf.at[:, block], rs_sem.at[level])
-        tile = half[block, yz // 16, rows((yz % 16) * 8, 8), :]
-        for i in range(NYZ - 1):
-            tile = tile + rsbuf[i, block]
-        if planes:
+        if level < 2:
+            for dy, dz in OTHERS:
+                k = lax.rem(y + dy, NY) * NZ + lax.rem(z + dz, NZ)
+                put(
+                    half.at[block, k // 16, rows((k % 16) * 8, 8), :],
+                    rsbuf.at[dy * NZ + dz - 1, block],
+                    send_sem.at[sem + 1], rs_sem.at[level], at(0, dy, dz),
+                )
+            sent(rsbuf.at[:, block], send_sem.at[sem + 1])
+            taken(rsbuf.at[:, block], rs_sem.at[level])
+            tile = half[block, yz // 16, rows((yz % 16) * 8, 8), :]
+            for i in range(NYZ - 1):
+                tile = tile + rsbuf[i, block]
+            piece = total.at[block, yz // 16, rows(c * 128 + (yz % 16) * 8, 8), :]
+            piece[...] = tile
+            for dy, dz in OTHERS:
+                put(piece, piece, send_sem.at[sem + 3], ag_sem.at[level], at(0, dy, dz))
+            sent(rsbuf.at[:, block], send_sem.at[sem + 3])
+            taken(rsbuf.at[:, block], ag_sem.at[level])
+        else:
             slot = level - 2
-            xbuf[slot, x] = tile
-            for d in planes:
-                to = (x // d % 2 * -2 * d + x + d) if len(planes) == 1 else lax.rem(x + d, NX)
+            peers = PLANES[level]
+            strip = 128 // (len(peers) + 1)
+            inbox = cellbuf.at[slot, pl.ds(0, len(peers)), :, pl.ds(0, strip), :]
+            whose = (lambda dx, dy: paired(dx, dy)) if level == 2 else (lambda dx, dy: at(dx, dy, 0))
+            index = (lambda to: to % 8) if level == 2 else (lambda to: to)
+            own = half[at_block, :, rows(index(cell) * strip, strip), :]
+            for dx, dy in peers:
+                to = whose(dx, dy)
                 put(
-                    xbuf.at[slot, x], xbuf.at[slot, x],
-                    send_sem.at[sem + 2], x_sem.at[slot], (to * NY + y, gene),
+                    half.at[at_block, :, rows(index(to[0]) * strip, strip), :],
+                    cellbuf.at[slot, dx * NY + dy - 1, :, pl.ds(0, strip), :],
+                    send_sem.at[sem + 1], rs_sem.at[level], to,
                 )
-            sent(xbuf.at[slot, pl.ds(0, len(planes))], send_sem.at[sem + 2])
-            taken(xbuf.at[slot, pl.ds(0, len(planes))], x_sem.at[slot])
-            if len(planes) == 1:
-                base = x - x % 2
-                tile = xbuf[slot, base] + xbuf[slot, base + 1]
-            else:
-                tile = (xbuf[slot, 0] + xbuf[slot, 1]) + (xbuf[slot, 2] + xbuf[slot, 3])
-        spot = rows(c * 128 + (yz % 16) * 8, 8)
-        total[block, yz // 16, spot, :] = tile
-
-        def collect(i, carry):
-            _, to = other(i)
-            piece = total.at[block, yz // 16, spot, :]
-            put(piece, piece, send_sem.at[sem + 3], ag_sem.at[level], to)
-            return carry
-
-        lax.fori_loop(1, NYZ, collect, 0)
-        sent(rsbuf.at[:, block], send_sem.at[sem + 3])
-        taken(rsbuf.at[:, block], ag_sem.at[level])
+            sent(inbox, send_sem.at[sem + 1])
+            taken(inbox, rs_sem.at[level])
+            for i in range(len(peers)):
+                own = own + cellbuf[slot, i, :, :strip, :]
+            share = zbuf.at[slot, z, :, pl.ds(0, strip), :]
+            share[...] = own
+            for dz in ALONG_Z:
+                put(share, share, send_sem.at[sem + 2], z_sem.at[slot], at(0, 0, dz))
+            inbox = zbuf.at[slot, pl.ds(0, NZ - 1), :, pl.ds(0, strip), :]
+            sent(inbox, send_sem.at[sem + 2])
+            taken(inbox, z_sem.at[slot])
+            own = zbuf[slot, 0, :, :strip, :]
+            for i in range(1, NZ):
+                own = own + zbuf[slot, i, :, :strip, :]
+            piece = total.at[at_block, :, rows(c * 128 + index(cell) * strip, strip), :]
+            piece[...] = own
+            for dx, dy in peers:
+                put(piece, piece, send_sem.at[sem + 3], ag_sem.at[level], whose(dx, dy))
+            inbox = cellbuf.at[slot, pl.ds(0, len(peers)), :, pl.ds(0, strip), :]
+            sent(inbox, send_sem.at[sem + 3])
+            taken(inbox, ag_sem.at[level])
         put(
             total.at[block, :, mine, :], total.at[block, :, mine, :],
             send_sem.at[sem + 4], cag_sem.at[level], sibling,
@@ -246,7 +281,8 @@
 
     for p in range(2):
         halves(part.at[p], dot(rx[2 * p].astype(BF16), rx[2 * p + 1].astype(BF16), TN))
-    reduced(0, 0, 2, ())
+    reduced(0, 0, 2)
+    load_mix.wait()
     taken(selfall.at[pl.ds(0, 3), :, pl.ds(0, 128), :], self_sem.at[3])
     put(
         selfall.at[:, :, mine, :], selfall.at[:, :, mine, :],
@@ -264,7 +300,7 @@
 
     lows, highs = split(low[...]), split(high[...])
     halves(part.at[2], dot3(lows, highs, TN))
-    reduced(1, 2, 1, ())
+    reduced(1, 2, 1)
     w = split(weights(1, grams[0], joined(total[2]), grams[1]))
     quad[...] = dot3(lows, left(w), NT) + dot3(highs, right(w), NT)
 
@@ -286,7 +322,7 @@
         taken(buf.at[0], pair_sem.at[slot])
         lows, highs = split(buf[0]), split(buf[1])
         halves(part.at[level + 1], dot3(lows, highs, TN))
-        reduced(level, level + 1, 1, (1,) if level == 2 else (1, 2, 3))
+        reduced(level, level + 1, 1)
         taken(pairself.at[slot, 0, :, pl.ds(0, 128), :], pself_sem.at[slot])
         across = pairself.at[slot, 1 - bit, :, mine, :]
         put(across, across, send_sem.at[30 + slot], pself_sem.at[2 + slot], sibling)
@@ -301,12 +337,25 @@
         if out is not None:
             out[...] = sketch
 
-    start = y * QUART + x % 2 * (2 * PART) + x // 2 * PART
-    here = final.at[rows(start, PART), :]
-    final[rows(start, PART), :] = sketch
-    for i in range(1, 16):
-        put(here, here, send_sem.at[32], fin_sem, (lax.rem(cell + i, 16), gene))
+    def chunk(cx, cy, part_of=0, count=PART):
+        return final.at[rows(cy * QUART + cx % 2 * (2 * PART) + cx // 2 * PART + part_of, count), :]
+
+    here = chunk(x, y)
+    here[...] = sketch
+    for d in ALONG_Y:
+        put(here, here, send_sem.at[32], finx_sem.at[d - 1], at(d, 0, 0))
+        put(here, here, send_sem.at[32], finy_sem.at[d - 1], at(0, d, 0))
     sent(final.at[pl.ds(0, 15 * PART), :], send_sem.at[32])
+    for d in (1, 3, 2):
+        cx, cy = lax.rem(x + NX - d, NX), lax.rem(y + NY - d, NY)
+        taken(here, finx_sem.at[d - 1])
+        first = chunk(cx, y, 0, PART // 2)
+        for e in ALONG_Y:
+            put(first, first, send_sem.at[32], fin_sem, at(0, e, 0))
+        taken(here, finy_sem.at[d - 1])
+        second = chunk(x, cy, PART // 2, PART // 2)
+        for e in ALONG_Y:
+            put(second, second, send_sem.at[32], fin_sem, at(e, 0, 0))
 
     gram = own_gram(w)
     norm = jnp.sqrt(jnp.sum(gram * gram, keepdims=True) + 1e-06)
@@ -328,7 +377,7 @@
     middle = split(1.5 * eye - 0.5 * dot3(zmat, ymat, NN))
     scaled = split(dot3(middle, zmat, NN) * (jnp.sqrt(F32(GENES)) / jnp.sqrt(norm)))
 
-    taken(final.at[pl.ds(0, 15 * PART), :], fin_sem)
+    taken(final.at[pl.ds(0, 9 * PART), :], fin_sem)
     hi, lo = split(final[...])
     fh[...] = hi
     fl[...] = lo
@@ -339,7 +388,7 @@
     sent(prodcore, send_sem.at[33])
     taken(prodcore, pr_sem.at[0])
     prodhalf[...] = prod[:, c] + prodcore[...]
-    for i in range(1, NZ):
+    for i in ALONG_Z:
         k = lax.rem(z + i, NZ)
         put(prodhalf.at[k], prodrs.at[i - 1], send_sem.at[34], pr_sem.at[1], (cell, k * 2 + c))
     sent(prodrs, send_sem.at[34])
@@ -349,12 +398,12 @@
     for i in range(NZ - 1):
         scores = scores + prodrs[i]
     sq[cell] = jnp.broadcast_to(jnp.sum(scores * scores, axis=1, keepdims=True), (16, 128))
-    for i in range(1, 16):
-        put(sq.at[cell], sq.at[cell], send_sem.at[35], sq_sem, (lax.rem(cell + i, 16), gene))
+    for dx, dy in PLANES[3]:
+        put(sq.at[cell], sq.at[cell], send_sem.at[35], sq_sem, at(dx, dy, 0))
     sent(sq.at[pl.ds(0, 15)], send_sem.at[35])
     taken(sq.at[pl.ds(0, 15)], sq_sem)
     spread = jnp.sum(sq[...], axis=0)[:, :1] * (1.0 / CELLS)
-    scores_ref[...] = (scores / jnp.sqrt(spread + 1e-05)).T
+    scores_ref[...] = scores / jnp.sqrt(spread + 1e-05)
     for like, sem in sends:
         taken(like, sem)
 
@@ -366,17 +415,18 @@
     def buf(*shape, kind=F32):
         return pltpu.VMEM(shape, kind)
 
-    return pl.pallas_call(
+    basis, scores = pl.pallas_call(
         kernel,
         out_shape=(
             jax.ShapeDtypeStruct((ELL, LOCAL), F32),
-            jax.ShapeDtypeStruct((ELL, 16), F32),
+            jax.ShapeDtypeStruct((16, ELL), F32),
         ),
-        in_specs=[vmem, vmem],
+        in_specs=[pl.BlockSpec(memory_space=pltpu.HBM)] * 2,
         out_specs=(vmem, vmem),
         scratch_shapes=[
+            buf(ELL, LOCAL, kind=BF16), buf(4, ELL, 2 * ELL, kind=BF16),
             buf(LOCAL, ELL), buf(NY, QUART, ELL), buf(5, 2, 256, 128), buf(5, 2, 128, 128),
-            buf(5, 2, 128, 128), buf(NYZ - 1, 5, 8, 128), buf(2, NX, 1, 8, 128), buf(5, 2, 256, 128),
+            buf(5, 2, 128, 128), buf(NYZ - 1, 5, 8, 128), buf(2, 15, 2, 16, 128), buf(2, NZ, 2, 16, 128), buf(5, 2, 256, 128),
             buf(2, 256, 128), buf(2, 128, 128), buf(2, 128, 128), buf(NZ - 1, 2, 16, 128),
             buf(NY, 2, 256, 128),
             buf(QUART, ELL), buf(QUART, ELL), buf(QUART, ELL), buf(2 * PART, ELL),
@@ -385,13 +435,14 @@
             buf(LOCAL, ELL, kind=BF16), buf(LOCAL, ELL, kind=BF16),
             buf(NZ, 2, 16, ELL), buf(NZ, 16, ELL), buf(NZ, 16, ELL), buf(NZ - 1, 16, ELL),
             buf(16, 16, 128),
-            dma((36,)), dma((4,)), dma((4,)), dma((4,)), dma((4,)), dma((2,)),
-            dma, dma((5,)), dma((2,)), dma((4,)), dma, dma((2,)), dma,
+            dma((2,)), dma((36,)), dma((4,)), dma((4,)), dma((4,)), dma((4,)), dma((2,)),
+            dma, dma((5,)), dma((2,)), dma((4,)), dma, dma((3,)), dma((3,)), dma((2,)), dma,
         ],
         compiler_params=pltpu.CompilerParams(
-            collective_id=0, has_side_effects=True, vmem_limit_bytes=52 * 2**20
+            collective_id=0, has_side_effects=True, vmem_limit_bytes=28 * 2**20
         ),
     )(expression, mixing)
+    return basis, scores.T
 
 
 def solution(mesh):

time: 173 us -> 151 us (0.87)
  Pallas kernels: 167 us -> 146 us
    pallas_call x1, Pallas kernels: 167 us -> 146 us  [on_device(): pl.pallas_call(kernel, out_shape=(jax.ShapeDtypeStruct((ELL, LOCAL), F32)...]
    unnamed x5 -> x6, local copies, waits for them, and re-layouts: 4.76 us -> 3.97 us
where the time goes in v2:
time: 151 us
  Pallas kernels  146 us (97%)
  local copies, waits for them, and re-layouts  3.97 us (3%)
    pallas_call x1, Pallas kernels, on_device(): pl.pallas_call(kernel, out_shape=(jax.ShapeDtypeStruct((ELL, LOCAL), F32)...  146 us
    unnamed x6, local copies, waits for them, and re-layouts  3.97 us

profile of v2, /device:TPU:1, one launch (start us, length us, event | category | flops | bytes accessed | tf_op | source)
XLA Modules:
  0.0 151.0 jit_solution(9800646720483351231)
XLA Ops:
  0.6 0.0 copy-start
  0.6 1.2 copy-done
  1.9 0.0 copy-start.1
  1.9 1.1 copy-done.1
  2.9 146.4 %shard_map.41 = (f32[256,1280]{1,0:T(8,128)S(1)}, f32[16,256]{1,0:T(8,128)S(1)}) custom-call(bf16[256,1280]{1,0:T(8,128)(2,1)S(1)} %copy-done.1, bf16[4,256,512]{2,1,0:T(8,128)(2,1)S(1)} %copy-done), custom_call_target="tpu_custom_call" | custom-call | tf_op jit(solution)/shard_map/pallas_call | solution.py:418
  149.4 1.1 copy.6
  150.4 0.6 copy.7
Async XLA Ops:
  0.6 1.2 copy-start
  1.9 1.1 copy-start.1

commit v3 on v2

--- a/solution.py
+++ b/solution.py
@@ -14,6 +14,7 @@
 LOCAL = GENES // 16
 QUART = LOCAL // NY
 PART = LOCAL // 16
+EARLY = PART // 2
 MESH = pl.DeviceIdType.MESH
 F32 = jnp.float32
 BF16 = jnp.bfloat16
@@ -71,13 +72,13 @@
 
 
 def kernel(
-    x_hbm, mix_hbm, basis_ref, scores_ref,
-    x_ref, mix_ref, xt, rx, part, corebuf, half, rsbuf, cellbuf, zbuf, total,
+    x_hbm, mix_hbm, basis_hbm, scores_ref,
+    x_ref, mix_ref, basis_ref, xt, rx, part, corebuf, half, rsbuf, cellbuf, zbuf, total,
     selfp, selfcore, selfhalf, selfrs, selfall,
-    low, high, quad, mid, pairbuf2, pairbuf3, pairself, final,
+    low, high, quad, mid, pairbuf2, pairbuf3, pairself, early, final,
     gh, gl, fh, fl, prod, prodcore, prodhalf, prodrs, sq,
     load_sem, send_sem, core_sem, rs_sem, ag_sem, cag_sem, z_sem,
-    a2a_sem, self_sem, pair_sem, pself_sem, fin_sem, finx_sem, finy_sem, pr_sem, sq_sem,
+    a2a_sem, self_sem, pair_sem, pself_sem, earlyx_sem, earlyy_sem, early_sem, fin_sem, finx_sem, finy_sem, pr_sem, sq_sem,
 ):
     cell, gene = lax.axis_index("cell"), lax.axis_index("gene")
     x, y = cell // NY, cell % NY
@@ -116,11 +117,12 @@
     def greet(to):
         pl.semaphore_signal(barrier, inc=1, device_id=to, device_id_type=MESH)
 
-    for dy, dz in OTHERS:
-        greet(at(0, dy, dz))
-    for dx, dy in PLANES[3]:
-        if dx:
-            greet(at(dx, dy, 0))
+    for d in ALONG_Y:
+        greet(at(0, d, 0))
+    for d in ALONG_Z:
+        greet(at(0, 0, d))
+    for d in ALONG_Y:
+        greet(at(d, 0, 0))
     greet(sibling)
     load_x.wait()
 
@@ -130,7 +132,7 @@
     rx[y] = xt[own, :]
     xb = x_ref[...]
     halves(selfp, dot(xb, xb, NT))
-    pl.semaphore_wait(barrier, NYZ - 1 + 12 + 1)
+    pl.semaphore_wait(barrier, NZ - 1 + NY - 1 + NX - 1 + 1)
 
     for i in ALONG_Y:
         q = lax.rem(y + i, NY)
@@ -181,7 +183,7 @@
 
     taken(rx.at[pl.ds(0, 3)], a2a_sem)
 
-    def reduced(level, at_block, count):
+    def reduced(level, at_block, count, scattering=None, summing=None, gathering=None):
         block = pl.ds(at_block, count)
         sem = 5 + 5 * level
         put(
@@ -200,6 +202,8 @@
                     send_sem.at[sem + 1], rs_sem.at[level], at(0, dy, dz),
                 )
             sent(rsbuf.at[:, block], send_sem.at[sem + 1])
+            if scattering is not None:
+                scattering()
             taken(rsbuf.at[:, block], rs_sem.at[level])
             tile = half[block, yz // 16, rows((yz % 16) * 8, 8), :]
             for i in range(NYZ - 1):
@@ -209,6 +213,8 @@
             for dy, dz in OTHERS:
                 put(piece, piece, send_sem.at[sem + 3], ag_sem.at[level], at(0, dy, dz))
             sent(rsbuf.at[:, block], send_sem.at[sem + 3])
+            if gathering is not None:
+                gathering()
             taken(rsbuf.at[:, block], ag_sem.at[level])
         else:
             slot = level - 2
@@ -226,6 +232,7 @@
                     send_sem.at[sem + 1], rs_sem.at[level], to,
                 )
             sent(inbox, send_sem.at[sem + 1])
+            scattering()
             taken(inbox, rs_sem.at[level])
             for i in range(len(peers)):
                 own = own + cellbuf[slot, i, :, :strip, :]
@@ -235,6 +242,8 @@
                 put(share, share, send_sem.at[sem + 2], z_sem.at[slot], at(0, 0, dz))
             inbox = zbuf.at[slot, pl.ds(0, NZ - 1), :, pl.ds(0, strip), :]
             sent(inbox, send_sem.at[sem + 2])
+            if summing is not None:
+                summing()
             taken(inbox, z_sem.at[slot])
             own = zbuf[slot, 0, :, :strip, :]
             for i in range(1, NZ):
@@ -245,6 +254,7 @@
                 put(piece, piece, send_sem.at[sem + 3], ag_sem.at[level], whose(dx, dy))
             inbox = cellbuf.at[slot, pl.ds(0, len(peers)), :, pl.ds(0, strip), :]
             sent(inbox, send_sem.at[sem + 3])
+            gathering()
             taken(inbox, ag_sem.at[level])
         put(
             total.at[block, :, mine, :], total.at[block, :, mine, :],
@@ -253,7 +263,7 @@
         sent(corebuf.at[block], send_sem.at[sem + 4])
         taken(corebuf.at[block], cag_sem.at[level])
 
-    def weights(level, lower, cross, upper):
+    def weights(level, lower, cross, upper, slot=0):
         gram = jnp.concatenate(
             [
                 jnp.concatenate([lower, cross], axis=1),
@@ -263,15 +273,15 @@
         )
         inv = 1.0 / jnp.sqrt(jnp.sum(gram * gram, keepdims=True) + 1e-06)
         hi, lo = split(gram)
-        gh[...] = hi
-        gl[...] = lo
+        gh[slot] = hi
+        gl[slot] = lo
         mix = mix_ref[level]
-        once = dot2(mix, (gh[...], gl[...]), NN)
-        twice = dot3(split(once), (gh[...], gl[...]), NN)
+        once = dot2(mix, (gh[slot], gl[slot]), NN)
+        twice = dot3(split(once), (gh[slot], gl[slot]), NN)
         return 0.5 * mix.astype(F32) + once * inv - (0.5 * twice) * (inv * inv)
 
-    def own_gram(w):
-        return dot3(split(dot3(w, (gh[...], gl[...]), NN)), w, NT)
+    def own_gram(w, slot=0):
+        return dot3(split(dot3(w, (gh[slot], gl[slot]), NN)), w, NT)
 
     def left(w):
         return w[0][:, :ELL], w[1][:, :ELL]
@@ -281,81 +291,101 @@
 
     for p in range(2):
         halves(part.at[p], dot(rx[2 * p].astype(BF16), rx[2 * p + 1].astype(BF16), TN))
-    reduced(0, 0, 2)
+
+    def swap_selves():
+        taken(selfall.at[pl.ds(0, 3), :, pl.ds(0, 128), :], self_sem.at[3])
+        put(
+            selfall.at[:, :, mine, :], selfall.at[:, :, mine, :],
+            send_sem.at[25], self_sem.at[4], sibling,
+        )
+        sent(selfall.at[:, :, pl.ds(0, 128), :], send_sem.at[25])
+
+    reduced(0, 0, 2, gathering=swap_selves)
     load_mix.wait()
-    taken(selfall.at[pl.ds(0, 3), :, pl.ds(0, 128), :], self_sem.at[3])
-    put(
-        selfall.at[:, :, mine, :], selfall.at[:, :, mine, :],
-        send_sem.at[25], self_sem.at[4], sibling,
-    )
-    sent(selfall.at[:, :, pl.ds(0, 128), :], send_sem.at[25])
     taken(selfall.at[:, :, pl.ds(0, 128), :], self_sem.at[4])
-    grams = []
+    kept = []
     for p, sketch in ((0, low), (1, high)):
-        w = split(weights(0, joined(selfall[2 * p]), joined(total[p]), joined(selfall[2 * p + 1])))
+        w = split(weights(0, joined(selfall[2 * p]), joined(total[p]), joined(selfall[2 * p + 1]), p))
         sketch[...] = dot2(rx[2 * p].astype(BF16), left(w), NT) + dot2(
             rx[2 * p + 1].astype(BF16), right(w), NT
         )
-        grams.append(own_gram(w))
+        kept.append(w)
 
     lows, highs = split(low[...]), split(high[...])
     halves(part.at[2], dot3(lows, highs, TN))
-    reduced(1, 2, 1)
+    grams = []
+    reduced(1, 2, 1, lambda: grams.extend(own_gram(kept[p], p) for p in range(2)))
     w = split(weights(1, grams[0], joined(total[2]), grams[1]))
-    quad[...] = dot3(lows, left(w), NT) + dot3(highs, right(w), NT)
-
-    for level, step, src, buf, out in ((2, 1, quad, pairbuf2, mid), (3, 2, mid, pairbuf3, None)):
+
+    def order(cx, cy):
+        return cy * 4 + cx % 2 * 2 + cx // 2
+
+    for level, step, src, buf in ((2, 1, quad, pairbuf2), (3, 2, mid, pairbuf3)):
         slot = level - 2
         bit = x // step % 2
         to = ((x + step * (1 - 2 * bit)) * NY + y, gene)
         count = buf.shape[1]
+        src[...] = dot3(lows, left(w), NT) + dot3(highs, right(w), NT)
         put(
             src.at[rows((1 - bit) * count, count), :], buf.at[bit],
             send_sem.at[26 + slot], pair_sem.at[slot], to,
         )
         sent(buf.at[0], send_sem.at[26 + slot])
         buf[bit] = src[rows(bit * count, count), :]
-        halves(pairself.at[slot, bit], own_gram(w))
-        share = pairself.at[slot, bit, :, mine, :]
-        put(share, share, send_sem.at[28 + slot], pself_sem.at[slot], to)
-        sent(pairself.at[slot, 0, :, pl.ds(0, 128), :], send_sem.at[28 + slot])
+        own = w
+
+        def scattering():
+            halves(pairself.at[slot, bit], own_gram(own))
+            share = pairself.at[slot, bit, :, mine, :]
+            put(share, share, send_sem.at[28 + slot], pself_sem.at[slot], to)
+            sent(pairself.at[slot, 0, :, pl.ds(0, 128), :], send_sem.at[28 + slot])
+
+        def summing():
+            here = early.at[:, rows(order(x, y) * EARLY, EARLY), :]
+            here[...] = buf[:, :EARLY, :]
+            for d in ALONG_Y:
+                put(here, here, send_sem.at[36], earlyx_sem.at[d - 1], at(d, 0, 0))
+                put(here, here, send_sem.at[36], earlyy_sem.at[d - 1], at(0, d, 0))
+            sent(final.at[pl.ds(0, 30 * EARLY), :], send_sem.at[36])
+
+        def gathering():
+            taken(pairself.at[slot, 0, :, pl.ds(0, 128), :], pself_sem.at[slot])
+            across = pairself.at[slot, 1 - bit, :, mine, :]
+            put(across, across, send_sem.at[30 + slot], pself_sem.at[2 + slot], sibling)
+            sent(pairself.at[slot, 0, :, pl.ds(0, 128), :], send_sem.at[30 + slot])
+            if level == 3:
+                for d in (1, 3, 2):
+                    cx, cy = lax.rem(x + NX - d, NX), lax.rem(y + NY - d, NY)
+                    taken(early.at[:, pl.ds(0, EARLY), :], earlyx_sem.at[d - 1])
+                    first = early.at[0, rows(order(cx, y) * EARLY, EARLY), :]
+                    for e in ALONG_Y:
+                        put(first, first, send_sem.at[36], early_sem, at(0, e, 0))
+                    taken(early.at[:, pl.ds(0, EARLY), :], earlyy_sem.at[d - 1])
+                    second = early.at[1, rows(order(x, cy) * EARLY, EARLY), :]
+                    for e in ALONG_Y:
+                        put(second, second, send_sem.at[36], early_sem, at(e, 0, 0))
+
         taken(buf.at[0], pair_sem.at[slot])
         lows, highs = split(buf[0]), split(buf[1])
         halves(part.at[level + 1], dot3(lows, highs, TN))
-        reduced(level, level + 1, 1)
-        taken(pairself.at[slot, 0, :, pl.ds(0, 128), :], pself_sem.at[slot])
-        across = pairself.at[slot, 1 - bit, :, mine, :]
-        put(across, across, send_sem.at[30 + slot], pself_sem.at[2 + slot], sibling)
-        sent(pairself.at[slot, 0, :, pl.ds(0, 128), :], send_sem.at[30 + slot])
+        reduced(level, level + 1, 1, scattering, summing if level == 3 else None, gathering)
         taken(pairself.at[slot, 0, :, pl.ds(0, 128), :], pself_sem.at[2 + slot])
         w = split(
             weights(
                 level, joined(pairself[slot, 0]), joined(total[level + 1]), joined(pairself[slot, 1])
             )
         )
-        sketch = dot3(lows, left(w), NT) + dot3(highs, right(w), NT)
-        if out is not None:
-            out[...] = sketch
-
-    def chunk(cx, cy, part_of=0, count=PART):
-        return final.at[rows(cy * QUART + cx % 2 * (2 * PART) + cx // 2 * PART + part_of, count), :]
-
-    here = chunk(x, y)
-    here[...] = sketch
+
+    def chunk(cx, cy, skip, count):
+        return final.at[pl.ds(pl.multiple_of(order(cx, cy) * PART + EARLY + skip, 8), count), :]
+
+    late = PART - EARLY
+    here = chunk(x, y, 0, late)
+    here[...] = (dot3(lows, left(w), NT) + dot3(highs, right(w), NT))[EARLY:]
     for d in ALONG_Y:
         put(here, here, send_sem.at[32], finx_sem.at[d - 1], at(d, 0, 0))
         put(here, here, send_sem.at[32], finy_sem.at[d - 1], at(0, d, 0))
-    sent(final.at[pl.ds(0, 15 * PART), :], send_sem.at[32])
-    for d in (1, 3, 2):
-        cx, cy = lax.rem(x + NX - d, NX), lax.rem(y + NY - d, NY)
-        taken(here, finx_sem.at[d - 1])
-        first = chunk(cx, y, 0, PART // 2)
-        for e in ALONG_Y:
-            put(first, first, send_sem.at[32], fin_sem, at(0, e, 0))
-        taken(here, finy_sem.at[d - 1])
-        second = chunk(x, cy, PART // 2, PART // 2)
-        for e in ALONG_Y:
-            put(second, second, send_sem.at[32], fin_sem, at(e, 0, 0))
+    sent(final.at[pl.ds(0, 15 * late), :], send_sem.at[32])
 
     gram = own_gram(w)
     norm = jnp.sqrt(jnp.sum(gram * gram, keepdims=True) + 1e-06)
@@ -367,6 +397,22 @@
     zmat = middle
     ymat = dot3(split(ymat), split(middle), NN)
 
+    for d in (1, 3, 2):
+        cx, cy = lax.rem(x + NX - d, NX), lax.rem(y + NY - d, NY)
+        taken(here, finx_sem.at[d - 1])
+        first = chunk(cx, y, 0, 24)
+        for e in ALONG_Y:
+            put(first, first, send_sem.at[32], fin_sem, at(0, e, 0))
+        taken(here, finy_sem.at[d - 1])
+        second = chunk(x, cy, 24, late - 24)
+        for e in ALONG_Y:
+            put(second, second, send_sem.at[32], fin_sem, at(e, 0, 0))
+
+    taken(final.at[pl.ds(0, 18 * EARLY), :], early_sem)
+    ahead = dot3(split(early[0]), left(w), NT) + dot3(split(early[1]), right(w), NT)
+    for k in range(16):
+        final[k * PART:k * PART + EARLY, :] = ahead[k * EARLY:(k + 1) * EARLY]
+
     def refine(step, carry):
         ymat, zmat = split(carry[0]), split(carry[1])
         middle = split(1.5 * eye - 0.5 * dot3(zmat, ymat, NN))
@@ -377,7 +423,7 @@
     middle = split(1.5 * eye - 0.5 * dot3(zmat, ymat, NN))
     scaled = split(dot3(middle, zmat, NN) * (jnp.sqrt(F32(GENES)) / jnp.sqrt(norm)))
 
-    taken(final.at[pl.ds(0, 9 * PART), :], fin_sem)
+    taken(final.at[pl.ds(0, 9 * late), :], fin_sem)
     hi, lo = split(final[...])
     fh[...] = hi
     fl[...] = lo
@@ -393,6 +439,8 @@
         put(prodhalf.at[k], prodrs.at[i - 1], send_sem.at[34], pr_sem.at[1], (cell, k * 2 + c))
     sent(prodrs, send_sem.at[34])
     basis_ref[...] = dot3(scaled, (fh[...], fl[...]), NT)
+    store_basis = pltpu.make_async_copy(basis_ref, basis_hbm, load_sem.at[0])
+    store_basis.start()
     taken(prodrs, pr_sem.at[1])
     scores = prodhalf[z]
     for i in range(NZ - 1):
@@ -404,6 +452,7 @@
     taken(sq.at[pl.ds(0, 15)], sq_sem)
     spread = jnp.sum(sq[...], axis=0)[:, :1] * (1.0 / CELLS)
     scores_ref[...] = scores / jnp.sqrt(spread + 1e-05)
+    store_basis.wait()
     for like, sem in sends:
         taken(like, sem)
 
@@ -422,24 +471,24 @@
             jax.ShapeDtypeStruct((16, ELL), F32),
         ),
         in_specs=[pl.BlockSpec(memory_space=pltpu.HBM)] * 2,
-        out_specs=(vmem, vmem),
+        out_specs=(pl.BlockSpec(memory_space=pltpu.HBM), vmem),
         scratch_shapes=[
-            buf(ELL, LOCAL, kind=BF16), buf(4, ELL, 2 * ELL, kind=BF16),
+            buf(ELL, LOCAL, kind=BF16), buf(4, ELL, 2 * ELL, kind=BF16), buf(ELL, LOCAL),
             buf(LOCAL, ELL), buf(NY, QUART, ELL), buf(5, 2, 256, 128), buf(5, 2, 128, 128),
             buf(5, 2, 128, 128), buf(NYZ - 1, 5, 8, 128), buf(2, 15, 2, 16, 128), buf(2, NZ, 2, 16, 128), buf(5, 2, 256, 128),
             buf(2, 256, 128), buf(2, 128, 128), buf(2, 128, 128), buf(NZ - 1, 2, 16, 128),
             buf(NY, 2, 256, 128),
             buf(QUART, ELL), buf(QUART, ELL), buf(QUART, ELL), buf(2 * PART, ELL),
-            buf(2, 2 * PART, ELL), buf(2, PART, ELL), buf(2, 2, 2, 256, 128), buf(LOCAL, ELL),
-            buf(2 * ELL, 2 * ELL, kind=BF16), buf(2 * ELL, 2 * ELL, kind=BF16),
+            buf(2, 2 * PART, ELL), buf(2, PART, ELL), buf(2, 2, 2, 256, 128), buf(2, 16 * EARLY, ELL), buf(LOCAL, ELL),
+            buf(2, 2 * ELL, 2 * ELL, kind=BF16), buf(2, 2 * ELL, 2 * ELL, kind=BF16),
             buf(LOCAL, ELL, kind=BF16), buf(LOCAL, ELL, kind=BF16),
             buf(NZ, 2, 16, ELL), buf(NZ, 16, ELL), buf(NZ, 16, ELL), buf(NZ - 1, 16, ELL),
             buf(16, 16, 128),
-            dma((2,)), dma((36,)), dma((4,)), dma((4,)), dma((4,)), dma((4,)), dma((2,)),
-            dma, dma((5,)), dma((2,)), dma((4,)), dma, dma((3,)), dma((3,)), dma((2,)), dma,
+            dma((2,)), dma((37,)), dma((4,)), dma((4,)), dma((4,)), dma((4,)), dma((2,)),
+            dma, dma((5,)), dma((2,)), dma((4,)), dma((3,)), dma((3,)), dma, dma, dma((3,)), dma((3,)), dma((2,)), dma,
         ],
         compiler_params=pltpu.CompilerParams(
-            collective_id=0, has_side_effects=True, vmem_limit_bytes=28 * 2**20
+            collective_id=0, has_side_effects=True, vmem_limit_bytes=62 * 2**20
         ),
     )(expression, mixing)
     return basis, scores.T

time: 151 us -> 148 us (0.980)
  Pallas kernels: 146 us -> 144 us
    pallas_call x1, Pallas kernels: 146 us -> 144 us  [on_device(): pl.pallas_call(kernel, out_shape=(jax.ShapeDtypeStruct((ELL, LOCAL), F32)...]
    unnamed x6 -> x4, local copies, waits for them, and re-layouts: 3.97 us -> 3.07 us
where the time goes in v3:
time: 148 us
  Pallas kernels  144 us (97%)
  local copies, waits for them, and re-layouts  3.07 us (2%)
    pallas_call x1, Pallas kernels, on_device(): pl.pallas_call(kernel, out_shape=(jax.ShapeDtypeStruct((ELL, LOCAL), F32)...  144 us
    unnamed x4, local copies, waits for them, and re-layouts  3.07 us

profile of v3, /device:TPU:1, one launch (start us, length us, event | category | flops | bytes accessed | tf_op | source)
XLA Modules:
  0.0 147.7 jit_solution(17130724579938010218)
XLA Ops:
  0.6 144.0 %shard_map.41 = (f32[256,1280]{1,0:T(8,128)}, f32[16,256]{1,0:T(8,128)}) custom-call(bf16[256,1280]{1,0:T(8,128)(2,1)} %x_hbm.1, bf16[4,256,512]{2,1,0:T(8,128)(2,1)} %mix_hbm.1), custom_call_target="tpu_custom_call" | custom-call | tf_op jit(solution)/shard_map/pallas_call | solution.py:467
  144.6 0.0 copy-start
  144.6 2.5 %copy.6 = f32[256,1280]{1,0:T(8,128)} copy(f32[256,1280]{1,0:T(8,128)} %get-tuple-element.8) | data formatting | bytes 2621440
  147.1 0.0 copy-done
  147.1 0.6 copy.7
Async XLA Ops:
  144.6 2.5 %copy-start = (f32[16,256]{1,0:T(8,128)S(1)}, f32[16,256]{1,0:T(8,128)}, u32[]{:S(2)}) copy-start(f32[16,256]{1,0:T(8,128)} %get-tuple-element.5) | copy-start | bytes 49156

commit v4 on v3

--- a/solution.py
+++ b/solution.py
@@ -9,6 +9,7 @@
 CELLS = 4096
 ELL = 256
 NS_ITERS = 8
+AHEAD = 3
 NY, NX, NZ = 4, 4, 8
 NYZ = NY * NZ
 LOCAL = GENES // 16
@@ -232,7 +233,6 @@
                     send_sem.at[sem + 1], rs_sem.at[level], to,
                 )
             sent(inbox, send_sem.at[sem + 1])
-            scattering()
             taken(inbox, rs_sem.at[level])
             for i in range(len(peers)):
                 own = own + cellbuf[slot, i, :, :strip, :]
@@ -332,13 +332,10 @@
         )
         sent(buf.at[0], send_sem.at[26 + slot])
         buf[bit] = src[rows(bit * count, count), :]
-        own = w
-
-        def scattering():
-            halves(pairself.at[slot, bit], own_gram(own))
-            share = pairself.at[slot, bit, :, mine, :]
-            put(share, share, send_sem.at[28 + slot], pself_sem.at[slot], to)
-            sent(pairself.at[slot, 0, :, pl.ds(0, 128), :], send_sem.at[28 + slot])
+        halves(pairself.at[slot, bit], own_gram(w))
+        share = pairself.at[slot, bit, :, mine, :]
+        put(share, share, send_sem.at[28 + slot], pself_sem.at[slot], to)
+        sent(pairself.at[slot, 0, :, pl.ds(0, 128), :], send_sem.at[28 + slot])
 
         def summing():
             here = early.at[:, rows(order(x, y) * EARLY, EARLY), :]
@@ -368,7 +365,7 @@
         taken(buf.at[0], pair_sem.at[slot])
         lows, highs = split(buf[0]), split(buf[1])
         halves(part.at[level + 1], dot3(lows, highs, TN))
-        reduced(level, level + 1, 1, scattering, summing if level == 3 else None, gathering)
+        reduced(level, level + 1, 1, None, summing if level == 3 else None, gathering)
         taken(pairself.at[slot, 0, :, pl.ds(0, 128), :], pself_sem.at[2 + slot])
         w = split(
             weights(
@@ -396,6 +393,13 @@
     middle = 1.5 * eye - 0.5 * ymat
     zmat = middle
     ymat = dot3(split(ymat), split(middle), NN)
+
+    def refine(step, carry):
+        ymat, zmat = split(carry[0]), split(carry[1])
+        middle = split(1.5 * eye - 0.5 * dot3(zmat, ymat, NN))
+        return dot3(ymat, middle, NN), dot3(middle, zmat, NN)
+
+    ymat, zmat = lax.fori_loop(0, AHEAD, refine, (ymat, zmat))
 
     for d in (1, 3, 2):
         cx, cy = lax.rem(x + NX - d, NX), lax.rem(y + NY - d, NY)
@@ -413,12 +417,7 @@
     for k in range(16):
         final[k * PART:k * PART + EARLY, :] = ahead[k * EARLY:(k + 1) * EARLY]
 
-    def refine(step, carry):
-        ymat, zmat = split(carry[0]), split(carry[1])
-        middle = split(1.5 * eye - 0.5 * dot3(zmat, ymat, NN))
-        return dot3(ymat, middle, NN), dot3(middle, zmat, NN)
-
-    ymat, zmat = lax.fori_loop(0, NS_ITERS - 2, refine, (ymat, zmat))
+    ymat, zmat = lax.fori_loop(AHEAD, NS_ITERS - 2, refine, (ymat, zmat))
     ymat, zmat = split(ymat), split(zmat)
     middle = split(1.5 * eye - 0.5 * dot3(zmat, ymat, NN))
     scaled = split(dot3(middle, zmat, NN) * (jnp.sqrt(F32(GENES)) / jnp.sqrt(norm)))

time: 148 us -> 145 us (0.980)
  Pallas kernels: 144 us -> 141 us
    pallas_call x1, Pallas kernels: 144 us -> 141 us  [on_device(): pl.pallas_call(kernel, out_shape=(jax.ShapeDtypeStruct((ELL, LOCAL), F32)...]
where the time goes in v4:
time: 145 us
  Pallas kernels  141 us (97%)
  local copies, waits for them, and re-layouts  3.07 us (2%)
    pallas_call x1, Pallas kernels, on_device(): pl.pallas_call(kernel, out_shape=(jax.ShapeDtypeStruct((ELL, LOCAL), F32)...  141 us
    unnamed x4, local copies, waits for them, and re-layouts  3.07 us

profile of v4, /device:TPU:1, one launch (start us, length us, event | category | flops | bytes accessed | tf_op | source)
XLA Modules:
  0.0 145.1 jit_solution(17188220410921554740)
XLA Ops:
  0.6 141.4 %shard_map.41 = (f32[256,1280]{1,0:T(8,128)}, f32[16,256]{1,0:T(8,128)}) custom-call(bf16[256,1280]{1,0:T(8,128)(2,1)} %x_hbm.1, bf16[4,256,512]{2,1,0:T(8,128)(2,1)} %mix_hbm.1), custom_call_target="tpu_custom_call" | custom-call | tf_op jit(solution)/shard_map/pallas_call | solution.py:466
  142.1 0.0 copy-start
  142.1 2.5 %copy.6 = f32[256,1280]{1,0:T(8,128)} copy(f32[256,1280]{1,0:T(8,128)} %get-tuple-element.8) | data formatting | bytes 2621440
  144.5 0.0 copy-done
  144.5 0.6 copy.7
Async XLA Ops:
  142.1 2.5 %copy-start = (f32[16,256]{1,0:T(8,128)S(1)}, f32[16,256]{1,0:T(8,128)}, u32[]{:S(2)}) copy-start(f32[16,256]{1,0:T(8,128)} %get-tuple-element.5) | copy-start | bytes 49156

commit v5 on v4

--- a/solution.py
+++ b/solution.py
@@ -77,7 +77,7 @@
     x_ref, mix_ref, basis_ref, xt, rx, part, corebuf, half, rsbuf, cellbuf, zbuf, total,
     selfp, selfcore, selfhalf, selfrs, selfall,
     low, high, quad, mid, pairbuf2, pairbuf3, pairself, early, final,
-    gh, gl, fh, fl, prod, prodcore, prodhalf, prodrs, sq,
+    stash, gh, gl, fh, fl, prod, prodcore, prodhalf, prodrs, sq,
     load_sem, send_sem, core_sem, rs_sem, ag_sem, cag_sem, z_sem,
     a2a_sem, self_sem, pair_sem, pself_sem, earlyx_sem, earlyy_sem, early_sem, fin_sem, finx_sem, finy_sem, pr_sem, sq_sem,
 ):
@@ -184,14 +184,16 @@
 
     taken(rx.at[pl.ds(0, 3)], a2a_sem)
 
-    def reduced(level, at_block, count, scattering=None, summing=None, gathering=None):
+    def reduced(level, at_block, count, cross, scattering=None, summing=None, gathering=None):
         block = pl.ds(at_block, count)
         sem = 5 + 5 * level
+        cross(1 - c)
         put(
             part.at[block, :, theirs, :], corebuf.at[block],
             send_sem.at[sem], core_sem.at[level], sibling,
         )
         sent(corebuf.at[block], send_sem.at[sem])
+        cross(c)
         taken(corebuf.at[block], core_sem.at[level])
         half[block] = part[block, :, mine, :] + corebuf[block]
         if level < 2:
@@ -263,20 +265,26 @@
         sent(corebuf.at[block], send_sem.at[sem + 4])
         taken(corebuf.at[block], cag_sem.at[level])
 
-    def weights(level, lower, cross, upper, slot=0):
-        gram = jnp.concatenate(
-            [
-                jnp.concatenate([lower, cross], axis=1),
-                jnp.concatenate([cross.T, upper], axis=1),
-            ],
-            axis=0,
-        )
-        inv = 1.0 / jnp.sqrt(jnp.sum(gram * gram, keepdims=True) + 1e-06)
-        hi, lo = split(gram)
-        gh[slot] = hi
-        gl[slot] = lo
+    def prepare(level, lower, upper, slot=0):
+        for at_row, gram in ((0, lower), (ELL, upper)):
+            spot = slice(at_row, at_row + ELL)
+            gh[slot, spot, spot], gl[slot, spot, spot] = split(gram)
         mix = mix_ref[level]
-        once = dot2(mix, (gh[slot], gl[slot]), NN)
+        first = dot2(mix[:, :ELL], (gh[slot, :ELL, :ELL], gl[slot, :ELL, :ELL]), NN)
+        second = dot2(mix[:, ELL:], (gh[slot, ELL:, ELL:], gl[slot, ELL:, ELL:]), NN)
+        squares = jnp.sum(lower * lower, keepdims=True) + jnp.sum(upper * upper, keepdims=True)
+        return first, second, squares
+
+    def weights(level, cross, ready, slot=0):
+        first, second, squares = ready
+        inv = 1.0 / jnp.sqrt(squares + 2.0 * jnp.sum(cross * cross, keepdims=True) + 1e-06)
+        over, under = split(cross), split(cross.T)
+        gh[slot, :ELL, ELL:], gl[slot, :ELL, ELL:] = over
+        gh[slot, ELL:, :ELL], gl[slot, ELL:, :ELL] = under
+        mix = mix_ref[level]
+        once = jnp.concatenate(
+            [first + dot2(mix[:, ELL:], under, NN), second + dot2(mix[:, :ELL], over, NN)], axis=1
+        )
         twice = dot3(split(once), (gh[slot], gl[slot]), NN)
         return 0.5 * mix.astype(F32) + once * inv - (0.5 * twice) * (inv * inv)
 
@@ -289,8 +297,40 @@
     def right(w):
         return w[0][:, ELL:], w[1][:, ELL:]
 
-    for p in range(2):
-        halves(part.at[p], dot(rx[2 * p].astype(BF16), rx[2 * p + 1].astype(BF16), TN))
+    def stashed(base, count):
+        at_rows = rows(base, count) if base is not None else pl.ds(0, count)
+        return (stash[0, at_rows, :], stash[1, at_rows, :]), (stash[2, at_rows, :], stash[3, at_rows, :])
+
+    def sketched(w, base, count):
+        lower, upper = stashed(base, count)
+        return dot3(lower, left(w), NT) + dot3(upper, right(w), NT)
+
+    def crossed(at_block, count):
+        def cross(side):
+            side_rows = rows(side * 128, 128)
+            lower = stash[0, :count, side_rows], stash[1, :count, side_rows]
+            block = dot3(lower, stashed(None, count)[1], TN)
+            part[at_block, 0, side_rows, :] = block[:, :128]
+            part[at_block, 1, side_rows, :] = block[:, 128:]
+
+        return cross
+
+    def keep(lower, upper):
+        count = lower.shape[0]
+        stash[0, :count], stash[1, :count] = split(lower)
+        stash[2, :count], stash[3, :count] = split(upper)
+
+    for i in range(NY):
+        stash[i] = rx[i].astype(BF16)
+
+    def cross_batches(side):
+        side_rows = rows(side * 128, 128)
+        for p in range(2):
+            block = dot(stash[2 * p, :, side_rows], stash[2 * p + 1], TN)
+            part[p, 0, side_rows, :] = block[:, :128]
+            part[p, 1, side_rows, :] = block[:, 128:]
+
+    ready = []
 
     def swap_selves():
         taken(selfall.at[pl.ds(0, 3), :, pl.ds(0, 128), :], self_sem.at[3])
@@ -299,23 +339,26 @@
             send_sem.at[25], self_sem.at[4], sibling,
         )
         sent(selfall.at[:, :, pl.ds(0, 128), :], send_sem.at[25])
-
-    reduced(0, 0, 2, gathering=swap_selves)
-    load_mix.wait()
-    taken(selfall.at[:, :, pl.ds(0, 128), :], self_sem.at[4])
+        load_mix.wait()
+        taken(selfall.at[:, :, pl.ds(0, 128), :], self_sem.at[4])
+        for p in range(2):
+            ready.append(prepare(0, joined(selfall[2 * p]), joined(selfall[2 * p + 1]), p))
+
+    reduced(0, 0, 2, cross_batches, gathering=swap_selves)
     kept = []
     for p, sketch in ((0, low), (1, high)):
-        w = split(weights(0, joined(selfall[2 * p]), joined(total[p]), joined(selfall[2 * p + 1]), p))
-        sketch[...] = dot2(rx[2 * p].astype(BF16), left(w), NT) + dot2(
-            rx[2 * p + 1].astype(BF16), right(w), NT
-        )
+        w = split(weights(0, joined(total[p]), ready[p], p))
+        sketch[...] = dot2(stash[2 * p], left(w), NT) + dot2(stash[2 * p + 1], right(w), NT)
         kept.append(w)
 
-    lows, highs = split(low[...]), split(high[...])
-    halves(part.at[2], dot3(lows, highs, TN))
+    keep(low[...], high[...])
     grams = []
-    reduced(1, 2, 1, lambda: grams.extend(own_gram(kept[p], p) for p in range(2)))
-    w = split(weights(1, grams[0], joined(total[2]), grams[1]))
+    reduced(
+        1, 2, 1, crossed(2, QUART),
+        scattering=lambda: grams.extend(own_gram(kept[p], p) for p in range(2)),
+        gathering=lambda: ready.append(prepare(1, *grams)),
+    )
+    w = split(weights(1, joined(total[2]), ready[-1]))
 
     def order(cx, cy):
         return cy * 4 + cx % 2 * 2 + cx // 2
@@ -325,13 +368,10 @@
         bit = x // step % 2
         to = ((x + step * (1 - 2 * bit)) * NY + y, gene)
         count = buf.shape[1]
-        src[...] = dot3(lows, left(w), NT) + dot3(highs, right(w), NT)
-        put(
-            src.at[rows((1 - bit) * count, count), :], buf.at[bit],
-            send_sem.at[26 + slot], pair_sem.at[slot], to,
-        )
+        src[...] = sketched(w, (1 - bit) * count, count)
+        put(src, buf.at[bit], send_sem.at[26 + slot], pair_sem.at[slot], to)
         sent(buf.at[0], send_sem.at[26 + slot])
-        buf[bit] = src[rows(bit * count, count), :]
+        buf[bit] = sketched(w, bit * count, count)
         halves(pairself.at[slot, bit], own_gram(w))
         share = pairself.at[slot, bit, :, mine, :]
         put(share, share, send_sem.at[28 + slot], pself_sem.at[slot], to)
@@ -361,24 +401,23 @@
                     second = early.at[1, rows(order(x, cy) * EARLY, EARLY), :]
                     for e in ALONG_Y:
                         put(second, second, send_sem.at[36], early_sem, at(e, 0, 0))
+            taken(pairself.at[slot, 0, :, pl.ds(0, 128), :], pself_sem.at[2 + slot])
+            ready.append(prepare(level, joined(pairself[slot, 0]), joined(pairself[slot, 1])))
 
         taken(buf.at[0], pair_sem.at[slot])
-        lows, highs = split(buf[0]), split(buf[1])
-        halves(part.at[level + 1], dot3(lows, highs, TN))
-        reduced(level, level + 1, 1, None, summing if level == 3 else None, gathering)
-        taken(pairself.at[slot, 0, :, pl.ds(0, 128), :], pself_sem.at[2 + slot])
-        w = split(
-            weights(
-                level, joined(pairself[slot, 0]), joined(total[level + 1]), joined(pairself[slot, 1])
-            )
-        )
+        keep(buf[0], buf[1])
+        reduced(
+            level, level + 1, 1, crossed(level + 1, count),
+            summing=summing if level == 3 else None, gathering=gathering,
+        )
+        w = split(weights(level, joined(total[level + 1]), ready[-1]))
 
     def chunk(cx, cy, skip, count):
         return final.at[pl.ds(pl.multiple_of(order(cx, cy) * PART + EARLY + skip, 8), count), :]
 
     late = PART - EARLY
     here = chunk(x, y, 0, late)
-    here[...] = (dot3(lows, left(w), NT) + dot3(highs, right(w), NT))[EARLY:]
+    here[...] = sketched(w, None, PART)[EARLY:]
     for d in ALONG_Y:
         put(here, here, send_sem.at[32], finx_sem.at[d - 1], at(d, 0, 0))
         put(here, here, send_sem.at[32], finy_sem.at[d - 1], at(0, d, 0))
@@ -444,12 +483,17 @@
     scores = prodhalf[z]
     for i in range(NZ - 1):
         scores = scores + prodrs[i]
-    sq[cell] = jnp.broadcast_to(jnp.sum(scores * scores, axis=1, keepdims=True), (16, 128))
+    squares = jnp.sum(scores * scores, axis=1, keepdims=True)
+    lane = lax.broadcasted_iota(jnp.int32, (8, 128), 1)
+    sq[cell] = jnp.where(
+        lane < 64, jnp.broadcast_to(squares[:8], (8, 128)), jnp.broadcast_to(squares[8:], (8, 128))
+    )
     for dx, dy in PLANES[3]:
         put(sq.at[cell], sq.at[cell], send_sem.at[35], sq_sem, at(dx, dy, 0))
     sent(sq.at[pl.ds(0, 15)], send_sem.at[35])
     taken(sq.at[pl.ds(0, 15)], sq_sem)
-    spread = jnp.sum(sq[...], axis=0)[:, :1] * (1.0 / CELLS)
+    squares = jnp.sum(sq[...], axis=0)
+    spread = jnp.concatenate([squares[:, :1], squares[:, 64:65]], axis=0) * (1.0 / CELLS)
     scores_ref[...] = scores / jnp.sqrt(spread + 1e-05)
     store_basis.wait()
     for like, sem in sends:
@@ -477,12 +521,13 @@
             buf(5, 2, 128, 128), buf(NYZ - 1, 5, 8, 128), buf(2, 15, 2, 16, 128), buf(2, NZ, 2, 16, 128), buf(5, 2, 256, 128),
             buf(2, 256, 128), buf(2, 128, 128), buf(2, 128, 128), buf(NZ - 1, 2, 16, 128),
             buf(NY, 2, 256, 128),
-            buf(QUART, ELL), buf(QUART, ELL), buf(QUART, ELL), buf(2 * PART, ELL),
+            buf(QUART, ELL), buf(QUART, ELL), buf(2 * PART, ELL), buf(PART, ELL),
             buf(2, 2 * PART, ELL), buf(2, PART, ELL), buf(2, 2, 2, 256, 128), buf(2, 16 * EARLY, ELL), buf(LOCAL, ELL),
+            buf(4, QUART, ELL, kind=BF16),
             buf(2, 2 * ELL, 2 * ELL, kind=BF16), buf(2, 2 * ELL, 2 * ELL, kind=BF16),
             buf(LOCAL, ELL, kind=BF16), buf(LOCAL, ELL, kind=BF16),
             buf(NZ, 2, 16, ELL), buf(NZ, 16, ELL), buf(NZ, 16, ELL), buf(NZ - 1, 16, ELL),
-            buf(16, 16, 128),
+            buf(16, 8, 128),
             dma((2,)), dma((37,)), dma((4,)), dma((4,)), dma((4,)), dma((4,)), dma((2,)),
             dma, dma((5,)), dma((2,)), dma((4,)), dma((3,)), dma((3,)), dma, dma, dma((3,)), dma((3,)), dma((2,)), dma,
         ],

time: 145 us -> 143 us (0.986)
  Pallas kernels: 141 us -> 139 us
    pallas_call x1, Pallas kernels: 141 us -> 139 us  [on_device(): pl.pallas_call(kernel, out_shape=(jax.ShapeDtypeStruct((ELL, LOCAL), F32)...]
where the time goes in v5:
time: 143 us; the launch traced here: 142 us
  Pallas kernels  139 us (97%)
  local copies, waits for them, and re-layouts  3.07 us (2%)
    pallas_call x1, Pallas kernels, on_device(): pl.pallas_call(kernel, out_shape=(jax.ShapeDtypeStruct((ELL, LOCAL), F32)...  139 us
    unnamed x4, local copies, waits for them, and re-layouts  3.07 us

profile of v5, /device:TPU:1, one launch (start us, length us, event | category | flops | bytes accessed | tf_op | source)
XLA Modules:
  0.0 142.4 jit_solution(12998631387522443882)
XLA Ops:
  0.6 138.7 %shard_map.41 = (f32[256,1280]{1,0:T(8,128)}, f32[16,256]{1,0:T(8,128)}) custom-call(bf16[256,1280]{1,0:T(8,128)(2,1)} %x_hbm.1, bf16[4,256,512]{2,1,0:T(8,128)(2,1)} %mix_hbm.1), custom_call_target="tpu_custom_call" | custom-call | tf_op jit(solution)/shard_map/pallas_call | solution.py:510
  139.4 0.0 copy-start
  139.4 2.5 %copy.6 = f32[256,1280]{1,0:T(8,128)} copy(f32[256,1280]{1,0:T(8,128)} %get-tuple-element.8) | data formatting | bytes 2621440
  141.8 0.0 copy-done
  141.8 0.6 copy.7
Async XLA Ops:
  139.4 2.5 %copy-start = (f32[16,256]{1,0:T(8,128)S(1)}, f32[16,256]{1,0:T(8,128)}, u32[]{:S(2)}) copy-start(f32[16,256]{1,0:T(8,128)} %get-tuple-element.5) | copy-start | bytes 49156

commit v6 on v5

--- a/solution.py
+++ b/solution.py
@@ -9,13 +9,13 @@
 CELLS = 4096
 ELL = 256
 NS_ITERS = 8
-AHEAD = 3
+AHEAD = 2
 NY, NX, NZ = 4, 4, 8
 NYZ = NY * NZ
 LOCAL = GENES // 16
 QUART = LOCAL // NY
 PART = LOCAL // 16
-EARLY = PART // 2
+EARLY = PART * 7 // 10
 MESH = pl.DeviceIdType.MESH
 F32 = jnp.float32
 BF16 = jnp.bfloat16
@@ -118,9 +118,11 @@
     def greet(to):
         pl.semaphore_signal(barrier, inc=1, device_id=to, device_id_type=MESH)
 
+    for d in ALONG_Z[:3]:
+        greet(at(0, 0, d))
     for d in ALONG_Y:
         greet(at(0, d, 0))
-    for d in ALONG_Z:
+    for d in ALONG_Z[3:]:
         greet(at(0, 0, d))
     for d in ALONG_Y:
         greet(at(d, 0, 0))
@@ -383,7 +385,7 @@
             for d in ALONG_Y:
                 put(here, here, send_sem.at[36], earlyx_sem.at[d - 1], at(d, 0, 0))
                 put(here, here, send_sem.at[36], earlyy_sem.at[d - 1], at(0, d, 0))
-            sent(final.at[pl.ds(0, 30 * EARLY), :], send_sem.at[36])
+            sent(early.at[:, pl.ds(0, 15 * EARLY), :], send_sem.at[36])
 
         def gathering():
             taken(pairself.at[slot, 0, :, pl.ds(0, 128), :], pself_sem.at[slot])
@@ -416,6 +418,7 @@
         return final.at[pl.ds(pl.multiple_of(order(cx, cy) * PART + EARLY + skip, 8), count), :]
 
     late = PART - EARLY
+    cut = (late // 8 + 1) // 2 * 8
     here = chunk(x, y, 0, late)
     here[...] = sketched(w, None, PART)[EARLY:]
     for d in ALONG_Y:
@@ -443,11 +446,11 @@
     for d in (1, 3, 2):
         cx, cy = lax.rem(x + NX - d, NX), lax.rem(y + NY - d, NY)
         taken(here, finx_sem.at[d - 1])
-        first = chunk(cx, y, 0, 24)
+        first = chunk(cx, y, 0, cut)
         for e in ALONG_Y:
             put(first, first, send_sem.at[32], fin_sem, at(0, e, 0))
         taken(here, finy_sem.at[d - 1])
-        second = chunk(x, cy, 24, late - 24)
+        second = chunk(x, cy, cut, late - cut)
         for e in ALONG_Y:
             put(second, second, send_sem.at[32], fin_sem, at(e, 0, 0))
 

time: 143 us -> 141 us (0.986)
  Pallas kernels: 139 us -> 137 us
    pallas_call x1, Pallas kernels: 139 us -> 137 us  [on_device(): pl.pallas_call(kernel, out_shape=(jax.ShapeDtypeStruct((ELL, LOCAL), F32)...]
where the time goes in v6:
time: 141 us
  Pallas kernels  137 us (97%)
  local copies, waits for them, and re-layouts  3.07 us (2%)
    pallas_call x1, Pallas kernels, on_device(): pl.pallas_call(kernel, out_shape=(jax.ShapeDtypeStruct((ELL, LOCAL), F32)...  137 us
    unnamed x4, local copies, waits for them, and re-layouts  3.07 us

profile of v6, /device:TPU:1, one launch (start us, length us, event | category | flops | bytes accessed | tf_op | source)
XLA Modules:
  0.0 140.8 jit_solution(180004774144321983)
XLA Ops:
  0.6 137.0 %shard_map.41 = (f32[256,1280]{1,0:T(8,128)}, f32[16,256]{1,0:T(8,128)}) custom-call(bf16[256,1280]{1,0:T(8,128)(2,1)} %x_hbm.1, bf16[4,256,512]{2,1,0:T(8,128)(2,1)} %mix_hbm.1), custom_call_target="tpu_custom_call" | custom-call | tf_op jit(solution)/shard_map/pallas_call | solution.py:513
  137.7 0.0 copy-start
  137.7 2.5 %copy.6 = f32[256,1280]{1,0:T(8,128)} copy(f32[256,1280]{1,0:T(8,128)} %get-tuple-element.8) | data formatting | bytes 2621440
  140.1 0.0 copy-done
  140.1 0.6 copy.7
Async XLA Ops:
  137.7 2.5 %copy-start = (f32[16,256]{1,0:T(8,128)S(1)}, f32[16,256]{1,0:T(8,128)}, u32[]{:S(2)}) copy-start(f32[16,256]{1,0:T(8,128)} %get-tuple-element.5) | copy-start | bytes 49156

commit v7 on v6

--- a/solution.py
+++ b/solution.py
@@ -10,6 +10,7 @@
 ELL = 256
 NS_ITERS = 8
 AHEAD = 2
+STRIPS = 8
 NY, NX, NZ = 4, 4, 8
 NYZ = NY * NZ
 LOCAL = GENES // 16
@@ -503,6 +504,30 @@
         taken(like, sem)
 
 
+def handed_on(basis_in, scores_in, basis_out, scores_out, held, held_scores, in_sem, out_sem):
+    count = STRIPS
+    strip = ELL // count
+    first = pltpu.make_async_copy(scores_in, held_scores, in_sem.at[count])
+    first.start()
+    reads = []
+    for i in range(count):
+        spot = pl.ds(i * strip, strip)
+        read = pltpu.make_async_copy(basis_in.at[spot, :], held.at[spot, :], in_sem.at[i])
+        read.start()
+        reads.append(read)
+    first.wait()
+    writes = [pltpu.make_async_copy(held_scores, scores_out, out_sem.at[count])]
+    writes[0].start()
+    for i in range(count):
+        spot = pl.ds(i * strip, strip)
+        reads[i].wait()
+        write = pltpu.make_async_copy(held.at[spot, :], basis_out.at[spot, :], out_sem.at[i])
+        write.start()
+        writes.append(write)
+    for write in writes:
+        write.wait()
+
+
 def on_device(expression, mixing):
     vmem = pl.BlockSpec(memory_space=pltpu.VMEM)
     dma = pltpu.SemaphoreType.DMA
@@ -538,6 +563,17 @@
             collective_id=0, has_side_effects=True, vmem_limit_bytes=62 * 2**20
         ),
     )(expression, mixing)
+    hbm = pl.BlockSpec(memory_space=pltpu.HBM)
+    basis, scores = pl.pallas_call(
+        handed_on,
+        out_shape=(
+            jax.ShapeDtypeStruct((ELL, LOCAL), F32),
+            jax.ShapeDtypeStruct((16, ELL), F32),
+        ),
+        in_specs=[hbm, hbm],
+        out_specs=(hbm, hbm),
+        scratch_shapes=[buf(ELL, LOCAL), buf(16, ELL), dma((STRIPS + 1,)), dma((STRIPS + 1,))],
+    )(basis, scores)
     return basis, scores.T
 
 

time: 141 us -> 140 us (level)
  local copies, waits for them, and re-layouts: 3.07 us -> 0 us
  Pallas kernels: 137 us -> 139 us
    unnamed x4 -> x0, local copies, waits for them, and re-layouts: 3.07 us -> none
    pallas_call x0 -> x1, Pallas kernels: none -> 2.24 us  [on_device(): pl.pallas_call(handed_on, out_shape=(jax.ShapeDtypeStruct((ELL, LOCAL), F...]
where the time goes in v7:
time: 140 us
  Pallas kernels  139 us (99%)
    pallas_call x1, Pallas kernels, on_device(): pl.pallas_call(kernel, out_shape=(jax.ShapeDtypeStruct((ELL, LOCAL), F32)...  137 us

profile of v7, /device:TPU:1, one launch (start us, length us, event | category | flops | bytes accessed | tf_op | source)
XLA Modules:
  0.0 140.1 jit_solution(17860869074754375265)
XLA Ops:
  0.6 137.0 %shard_map.41 = (f32[256,1280]{1,0:T(8,128)}, f32[16,256]{1,0:T(8,128)}) custom-call(bf16[256,1280]{1,0:T(8,128)(2,1)} %x_hbm.1, bf16[4,256,512]{2,1,0:T(8,128)(2,1)} %mix_hbm.1), custom_call_target="tpu_custom_call" | custom-call | tf_op jit(solution)/shard_map/pallas_call | solution.py:538
  137.7 2.2 %shard_map.42 = (f32[256,1280]{1,0:T(8,128)}, f32[16,256]{1,0:T(8,128)}) custom-call(f32[256,1280]{1,0:T(8,128)} %get-tuple-element.6.basis_in, f32[16,256]{1,0:T(8,128)} %get-tuple-element.7.scores_in), custom_call_target="tpu_custom_call" | custom-call | tf_op jit(solution)/shard_map/pallas_call | solution.py:567

commit v8 on v7

--- a/solution.py
+++ b/solution.py
@@ -10,7 +10,7 @@
 ELL = 256
 NS_ITERS = 8
 AHEAD = 2
-STRIPS = 8
+STRIPS = 4
 NY, NX, NZ = 4, 4, 8
 NYZ = NY * NZ
 LOCAL = GENES // 16

time: 140 us -> 140 us (level)
  no operation moved by 1% of the time
where the time goes in v8:
time: 140 us
  Pallas kernels  139 us (99%)
    pallas_call x1, Pallas kernels, on_device(): pl.pallas_call(kernel, out_shape=(jax.ShapeDtypeStruct((ELL, LOCAL), F32)...  137 us

profile of v8, /device:TPU:1, one launch (start us, length us, event | category | flops | bytes accessed | tf_op | source)
XLA Modules:
  0.0 140.0 jit_solution(9482440460039583617)
XLA Ops:
  0.6 137.0 %shard_map.41 = (f32[256,1280]{1,0:T(8,128)}, f32[16,256]{1,0:T(8,128)}) custom-call(bf16[256,1280]{1,0:T(8,128)(2,1)} %x_hbm.1, bf16[4,256,512]{2,1,0:T(8,128)(2,1)} %mix_hbm.1), custom_call_target="tpu_custom_call" | custom-call | tf_op jit(solution)/shard_map/pallas_call | solution.py:538
  137.7 2.1 %shard_map.42 = (f32[256,1280]{1,0:T(8,128)}, f32[16,256]{1,0:T(8,128)}) custom-call(f32[256,1280]{1,0:T(8,128)} %get-tuple-element.6.basis_in, f32[16,256]{1,0:T(8,128)} %get-tuple-element.7.scores_in), custom_call_target="tpu_custom_call" | custom-call | tf_op jit(solution)/shard_map/pallas_call | solution.py:567
